TPU v7x, 256 devices: a whole 4x4x8 slice. The times are simulated.
256 devices in a mesh: elem: 64 (over x, z, core), sub: 4 (over y).
Axes of the slice: x: 4, y: 4, z: 8, core: 2. Of those that a mesh axis runs over, the one named last changes fastest.
Arguments:
- velocity: float32 [3, 512, 64, 128], P(None, 'elem', 'sub'), may hold values from -6 to 6
Outputs:
- advected: float32 [3, 512, 64, 128], P(None, 'elem', 'sub')
- pressure: float32 [512, 64, 128], P('elem', 'sub')
All inputs are finite; a program needn't handle non-finite values.
Results may differ from a plain program's by a relative error of at most 0.00021.
Values sent between devices are 32-bit elements; how exact they have to be, the bound alone decides.
A program may use at most 128 MiB of HBM per device.

v0:
```python
import jax
import jax.numpy as jnp
import numpy as np
from jax import lax
from jax.sharding import PartitionSpec as P

POINTS = 8
SUBSTEPS = 3
MG_ITERS = 3
COARSE_ITERS = 4


TIME_STEP = 0.005
SHIFT_COEF = 0.05
RELAXATION = 0.6
SOURCE_GAIN = 20.0


def extended(block, sides, width):
    for axis, dim in sides:
        count = lax.axis_size(axis)
        forward = [(i, i + 1) for i in range(count - 1)]
        forward.append((count - 1, 0))
        backward = [(target, source) for source, target in forward]
        low = lax.ppermute(
            lax.slice_in_dim(block, block.shape[dim] - width, None, axis=dim), axis, forward
        )
        high = lax.ppermute(lax.slice_in_dim(block, 0, width, axis=dim), axis, backward)
        block = jnp.concatenate([low, block, high], axis=dim)
    return block


def legendre_last(points, degree):
    previous = points * 0.0 + 1.0
    current = points + 0.0
    for level in range(2, degree + 1):
        following = ((2 * level - 1) * points * current - (level - 1) * previous) / level
        previous = current
        current = following
    return (previous, current)


def gll_tables(count):
    degree = count - 1
    points = -np.cos(np.pi * np.arange(count) / degree)
    for sweep in range(100):
        before_last, last_value = legendre_last(points, degree)
        points = points - (points * last_value - before_last) / (count * last_value)
    before_last, legendre = legendre_last(points, degree)
    weights = 2.0 / (degree * (degree + 1) * legendre**2)
    spacing = points[:, None] - points[None, :] + np.eye(count)
    matrix = legendre[:, None] / (legendre[None, :] * spacing) * (1.0 - np.eye(count))
    matrix[0, 0] = -degree * (degree + 1) / 4.0
    matrix[degree, degree] = degree * (degree + 1) / 4.0
    return (points, weights, matrix)


def apply_axis(field, axis, matrix):
    table = jnp.asarray(matrix, jnp.float32)
    out_count, in_count = matrix.shape
    layout = field.shape
    blocks = layout[axis] // in_count
    split = layout[:axis] + (blocks, in_count) + layout[axis + 1 :]
    forms = {1: "ij,kejxy->keixy", 2: "ij,kzejy->kzeiy", 3: "ij,kzxej->kzxei"}
    result = jnp.einsum(forms[axis], table, field.reshape(split), precision=lax.Precision.HIGHEST)
    return result.reshape(layout[:axis] + (blocks * out_count,) + layout[axis + 1 :])


def weight_field(layout, weights):
    count = weights.shape[0]
    along_z = np.tile(weights, layout[1] // count)
    along_x = np.tile(weights, layout[2] // count)
    along_y = np.tile(weights, layout[3] // count)
    table = along_z[:, None, None] * along_x[None, :, None] * along_y[None, None, :] / 8.0
    return jnp.asarray(table[None], jnp.float32)


def add_faces(padded, axis, count):
    length = padded.shape[axis] - 2
    center = lax.slice_in_dim(padded, 1, length + 1, axis=axis)
    after = lax.slice_in_dim(padded, 2, length + 2, axis=axis)
    before = lax.slice_in_dim(padded, 0, length, axis=axis)
    position = lax.broadcasted_iota(jnp.int32, center.shape, axis) % count
    return (
        center
        + jnp.where(position == count - 1, after, 0.0)
        + jnp.where(position == 0, before, 0.0)
    )


def wall_faces(field, count):
    padded = jnp.pad(field, ((0, 0), (0, 0), (0, 0), (1, 1)))
    return add_faces(padded, 3, count)


def share_fine(field):
    padded = extended(field, (("elem", 1),), 1)
    summed = add_faces(padded, 1, POINTS)
    padded = extended(summed, (("sub", 2),), 1)
    summed = add_faces(padded, 2, POINTS)
    return wall_faces(summed, POINTS)


def share_coarse(field):
    padded = extended(field, (("elem", 1), ("sub", 2)), 1)
    summed = add_faces(add_faces(padded, 1, 2), 2, 2)
    return wall_faces(summed, 2)


def local_operator(field, mass_local, matrix):
    total = SHIFT_COEF * mass_local * field
    for axis in (1, 2, 3):
        slope = apply_axis(field, axis, matrix)
        total = total + 4.0 * apply_axis(mass_local * slope, axis, matrix.T)
    return total


def local_diagonal(mass_local, matrix):
    total = SHIFT_COEF * mass_local
    for axis in (1, 2, 3):
        total = total + 4.0 * apply_axis(mass_local, axis, (matrix * matrix).T)
    return total


def conjugate(right_side, operator, inner):
    solution = jnp.zeros_like(right_side)
    residual = right_side
    direction = right_side
    norm_now = inner(residual, residual)
    for sweep in range(COARSE_ITERS):
        image = operator(direction)
        alpha = norm_now / inner(direction, image)
        solution = solution + alpha * direction
        residual = residual - alpha * image
        norm_next = inner(residual, residual)
        direction = residual + norm_next / norm_now * direction
        norm_now = norm_next
    return solution


def shards(velocity):
    abscissae, weights, matrix = gll_tables(POINTS)
    coarse_xi, coarse_weights, coarse_matrix = gll_tables(2)
    lift = np.stack([(1.0 - abscissae) / 2.0, (1.0 + abscissae) / 2.0], axis=1)
    layout = (1,) + velocity.shape[1:]
    mass_local = weight_field(layout, weights)
    setup = share_fine(
        jnp.concatenate(
            [mass_local, jnp.ones(layout, jnp.float32), local_diagonal(mass_local, matrix)], 0
        )
    )
    mass_sum = setup[0:1]
    multiplicity = setup[1:2]
    diagonal = setup[2:3]
    for sub_step in range(SUBSTEPS):
        term = jnp.zeros_like(velocity)
        for axis in (1, 2, 3):
            term = term + velocity[axis - 1 : axis] * apply_axis(velocity, axis, matrix)
        term = 2.0 * mass_local * term
        velocity = velocity - TIME_STEP * share_fine(term) / mass_sum
    divergence = jnp.zeros(layout, jnp.float32)
    for axis in (1, 2, 3):
        divergence = divergence + apply_axis(velocity[axis - 1 : axis], axis, matrix)
    source = -SOURCE_GAIN * share_fine(mass_local * divergence)
    coarse_layout = (1, layout[1] // POINTS * 2, layout[2] // POINTS * 2, layout[3] // POINTS * 2)
    coarse_mass = jnp.full(coarse_layout, 0.125, jnp.float32)
    coarse_count = share_coarse(jnp.ones(coarse_layout, jnp.float32))

    def coarse_apply(field):
        return share_coarse(local_operator(field, coarse_mass, coarse_matrix))

    def coarse_inner(left_side, right_part):
        return lax.psum(jnp.sum(left_side * right_part / coarse_count), ("elem", "sub"))

    def fine_apply(field):
        return share_fine(local_operator(field, mass_local, matrix))

    pressure = jnp.zeros(layout, jnp.float32)
    for cycle in range(MG_ITERS):
        residual = source if cycle == 0 else source - fine_apply(pressure)
        pressure = pressure + RELAXATION * residual / diagonal
        residual = source - fine_apply(pressure)
        reduced = residual / multiplicity
        for axis in (1, 2, 3):
            reduced = apply_axis(reduced, axis, lift.T)
        correction = conjugate(share_coarse(reduced), coarse_apply, coarse_inner)
        for axis in (1, 2, 3):
            correction = apply_axis(correction, axis, lift)
        pressure = pressure + correction
        residual = source - fine_apply(pressure)
        pressure = pressure + RELAXATION * residual / diagonal
    return (velocity, pressure[0])


def solution(mesh):
    return jax.shard_map(
        shards,
        mesh=mesh,
        in_specs=(P(None, "elem", "sub", None),),
        out_specs=(P(None, "elem", "sub", None), P("elem", "sub", None)),
        check_vma=False,
    )
```

profile of v0, /device:TPU:1, one launch (start us, length us, event | category | flops | bytes accessed | tf_op | source)
XLA Modules:
  0.0 2011.9 jit_solution(11436574513794726038)
XLA Ops:
  0.6 3.1 collective-permute-start.5
  12.1 4.4 collective-permute-start
  21.2 3.1 collective-permute-start.2
  30.4 7.3 collective-permute-start.8
  47.6 6.3 collective-permute-start.12
  58.3 5.9 collective-permute-start.29
  66.2 4.9 collective-permute-start.16
  79.5 6.5 collective-permute-start.20
  87.3 2.9 collective-permute-start.22
  92.7 6.2 collective-permute-start.25
  99.7 4.0 collective-permute-done.24
  103.7 3.0 collective-permute-start.27
  107.5 2.9 collective-permute-done.26
  112.0 7.2 collective-permute-start.33
  126.7 75.6 %all-reduce.31 = (f32[]{:T(128)}, f32[]{:T(128)}) all-reduce(f32[]{:T(128)} %get-tuple-element.11, f32[]{:T(128)} %get-tuple-element.10), channel_id=1, replica_groups=mesh['elem'=64,'sub'=4] {'elem','sub'}, use_global_device_ids=true, to_apply=%region_1.2 | all-reduce | flops 2 | bytes 16 | tf_op jit(solution)/shard_map/psum | solution.py:173
  204.3 74.2 %psum.170 = f32[]{:T(128)} all-reduce(f32[]{:T(128)} %fusion.537), channel_id=1, replica_groups=mesh['elem'=64,'sub'=4] {'elem','sub'}, use_global_device_ids=true, to_apply=%region_5.6 | all-reduce | flops 1 | bytes 8 | tf_op jit(solution)/shard_map/psum | solution.py:173
  291.6 76.4 %psum.171 = f32[]{:T(128)} all-reduce(f32[]{:T(128)} %get-tuple-element.36), channel_id=1, replica_groups=mesh['elem'=64,'sub'=4] {'elem','sub'}, use_global_device_ids=true, to_apply=%region_7.8 | all-reduce | flops 1 | bytes 8 | tf_op jit(solution)/shard_map/psum | solution.py:173
  369.9 74.2 %psum.172 = f32[]{:T(128)} all-reduce(f32[]{:T(128)} %get-tuple-element.34), channel_id=1, replica_groups=mesh['elem'=64,'sub'=4] {'elem','sub'}, use_global_device_ids=true, to_apply=%region_9.10 | all-reduce | flops 1 | bytes 8 | tf_op jit(solution)/shard_map/psum | solution.py:173
  453.3 2.8 collective-permute-done.42
  457.0 76.1 %psum.173 = f32[]{:T(128)} all-reduce(f32[]{:T(128)} %get-tuple-element.32), channel_id=1, replica_groups=mesh['elem'=64,'sub'=4] {'elem','sub'}, use_global_device_ids=true, to_apply=%region_11.12 | all-reduce | flops 1 | bytes 8 | tf_op jit(solution)/shard_map/psum | solution.py:173
  535.0 74.2 %psum.174 = f32[]{:T(128)} all-reduce(f32[]{:T(128)} %fusion.539), channel_id=1, replica_groups=mesh['elem'=64,'sub'=4] {'elem','sub'}, use_global_device_ids=true, to_apply=%region_13.14 | all-reduce | flops 1 | bytes 8 | tf_op jit(solution)/shard_map/psum | solution.py:173
  622.0 76.3 %psum.175 = f32[]{:T(128)} all-reduce(f32[]{:T(128)} %fusion.557), channel_id=1, replica_groups=mesh['elem'=64,'sub'=4] {'elem','sub'}, use_global_device_ids=true, to_apply=%region_15.16 | all-reduce | flops 1 | bytes 8 | tf_op jit(solution)/shard_map/psum | solution.py:173
  721.6 2.9 collective-permute-start.54
  729.3 5.1 collective-permute-start.56
  741.3 6.3 collective-permute-start.61
  748.5 3.9 collective-permute-done.60
  755.9 2.9 collective-permute-done.62
  760.4 7.2 collective-permute-start.65
  774.2 76.9 %all-reduce.30 = (f32[]{:T(128)}, f32[]{:T(128)}) all-reduce(f32[]{:T(128)} %get-tuple-element.9, f32[]{:T(128)} %get-tuple-element.8), channel_id=1, replica_groups=mesh['elem'=64,'sub'=4] {'elem','sub'}, use_global_device_ids=true, to_apply=%region_17.18 | all-reduce | flops 2 | bytes 16 | tf_op jit(solution)/shard_map/psum | solution.py:173
  853.1 74.2 %psum.178 = f32[]{:T(128)} all-reduce(f32[]{:T(128)} %fusion.541), channel_id=1, replica_groups=mesh['elem'=64,'sub'=4] {'elem','sub'}, use_global_device_ids=true, to_apply=%region_21.22 | all-reduce | flops 1 | bytes 8 | tf_op jit(solution)/shard_map/psum | solution.py:173
  940.2 76.1 %psum.179 = f32[]{:T(128)} all-reduce(f32[]{:T(128)} %get-tuple-element.29), channel_id=1, replica_groups=mesh['elem'=64,'sub'=4] {'elem','sub'}, use_global_device_ids=true, to_apply=%region_23.24 | all-reduce | flops 1 | bytes 8 | tf_op jit(solution)/shard_map/psum | solution.py:173
  1018.3 74.2 %psum.180 = f32[]{:T(128)} all-reduce(f32[]{:T(128)} %get-tuple-element.27), channel_id=1, replica_groups=mesh['elem'=64,'sub'=4] {'elem','sub'}, use_global_device_ids=true, to_apply=%region_25.26 | all-reduce | flops 1 | bytes 8 | tf_op jit(solution)/shard_map/psum | solution.py:173
  1105.4 76.1 %psum.181 = f32[]{:T(128)} all-reduce(f32[]{:T(128)} %get-tuple-element.25), channel_id=1, replica_groups=mesh['elem'=64,'sub'=4] {'elem','sub'}, use_global_device_ids=true, to_apply=%region_27.28 | all-reduce | flops 1 | bytes 8 | tf_op jit(solution)/shard_map/psum | solution.py:173
  1183.4 74.4 %psum.182 = f32[]{:T(128)} all-reduce(f32[]{:T(128)} %fusion.543), channel_id=1, replica_groups=mesh['elem'=64,'sub'=4] {'elem','sub'}, use_global_device_ids=true, to_apply=%region_29.30 | all-reduce | flops 1 | bytes 8 | tf_op jit(solution)/shard_map/psum | solution.py:173
  1270.6 76.1 %psum.183 = f32[]{:T(128)} all-reduce(f32[]{:T(128)} %fusion.558), channel_id=1, replica_groups=mesh['elem'=64,'sub'=4] {'elem','sub'}, use_global_device_ids=true, to_apply=%region_31.32 | all-reduce | flops 1 | bytes 8 | tf_op jit(solution)/shard_map/psum | solution.py:173
  1377.9 5.1 collective-permute-start.88
  1389.7 6.8 collective-permute-start.93
  1397.3 3.8 collective-permute-done.92
  1401.1 2.8 collective-permute-start.95
  1404.7 2.9 collective-permute-done.94
  1409.2 7.2 collective-permute-start.97
  1422.5 76.9 %all-reduce.29 = (f32[]{:T(128)}, f32[]{:T(128)}) all-reduce(f32[]{:T(128)} %get-tuple-element.7, f32[]{:T(128)} %get-tuple-element.6), channel_id=1, replica_groups=mesh['elem'=64,'sub'=4] {'elem','sub'}, use_global_device_ids=true, to_apply=%region_33.34 | all-reduce | flops 2 | bytes 16 | tf_op jit(solution)/shard_map/psum | solution.py:173
  1501.5 74.2 %psum.186 = f32[]{:T(128)} all-reduce(f32[]{:T(128)} %fusion.545), channel_id=1, replica_groups=mesh['elem'=64,'sub'=4] {'elem','sub'}, use_global_device_ids=true, to_apply=%region_37.38 | all-reduce | flops 1 | bytes 8 | tf_op jit(solution)/shard_map/psum | solution.py:173
  1588.6 76.1 %psum.187 = f32[]{:T(128)} all-reduce(f32[]{:T(128)} %get-tuple-element.22), channel_id=1, replica_groups=mesh['elem'=64,'sub'=4] {'elem','sub'}, use_global_device_ids=true, to_apply=%region_39.40 | all-reduce | flops 1 | bytes 8 | tf_op jit(solution)/shard_map/psum | solution.py:173
  1666.7 74.4 %psum.188 = f32[]{:T(128)} all-reduce(f32[]{:T(128)} %get-tuple-element.20), channel_id=1, replica_groups=mesh['elem'=64,'sub'=4] {'elem','sub'}, use_global_device_ids=true, to_apply=%region_41.42 | all-reduce | flops 1 | bytes 8 | tf_op jit(solution)/shard_map/psum | solution.py:173
  1753.9 76.1 %psum.189 = f32[]{:T(128)} all-reduce(f32[]{:T(128)} %get-tuple-element.18), channel_id=1, replica_groups=mesh['elem'=64,'sub'=4] {'elem','sub'}, use_global_device_ids=true, to_apply=%region_43.44 | all-reduce | flops 1 | bytes 8 | tf_op jit(solution)/shard_map/psum | solution.py:173
  1831.9 74.2 %psum.190 = f32[]{:T(128)} all-reduce(f32[]{:T(128)} %fusion.547), channel_id=1, replica_groups=mesh['elem'=64,'sub'=4] {'elem','sub'}, use_global_device_ids=true, to_apply=%region_45.46 | all-reduce | flops 1 | bytes 8 | tf_op jit(solution)/shard_map/psum | solution.py:173
  1919.0 76.3 %psum.191 = f32[]{:T(128)} all-reduce(f32[]{:T(128)} %fusion.559), channel_id=1, replica_groups=mesh['elem'=64,'sub'=4] {'elem','sub'}, use_global_device_ids=true, to_apply=%region_47.48 | all-reduce | flops 1 | bytes 8 | tf_op jit(solution)/shard_map/psum | solution.py:173
  (803 shorter events, 269.3 us)
Async XLA Ops:
  0.6 15.9 collective-permute-start.5
  3.7 12.8 collective-permute-start.4
  10.5 6.5 collective-permute-start.1
  12.1 5.3 collective-permute-start
  18.3 6.0 collective-permute-start.7
  19.7 4.7 collective-permute-start.6
  21.2 3.9 collective-permute-start.2
  30.3 8.0 collective-permute-start.9
  30.4 8.1 collective-permute-start.8
  38.6 4.7 collective-permute-start.11
  39.4 3.9 collective-permute-start.10
  47.6 7.0 collective-permute-start.13
  47.6 7.1 collective-permute-start.12
  54.9 9.3 collective-permute-start.15
  56.1 8.1 collective-permute-start.14
  58.3 60.9 %collective-permute-start.29 = (f32[1,1,4,32]{3,1,2,0:T(1,128)S(1)}, f32[1,1,4,32]{3,1,2,0:T(1,128)S(1)}, u32[]{:S(2)}, u32[]{:S(2)}) collective-permute-start(f32[1,1,4,32]{3,1,2,0:T(1,128)S(1)} %broadcast.1574), channel_id=1, source_target_pairs={{4,0},{8,4},{12,8},{16,12},{20,16},{24,20},{28,24},{32,28},{36,32}... | collective-permute-start | bytes 1544 | tf_op jit(solution)/shard_map/ppermute | solution.py:28
  64.2 55.0 %collective-permute-start.28 = (f32[1,1,4,32]{3,1,2,0:T(1,128)S(1)}, f32[1,1,4,32]{3,1,2,0:T(1,128)S(1)}, u32[]{:S(2)}, u32[]{:S(2)}) collective-permute-start(f32[1,1,4,32]{3,1,2,0:T(1,128)S(1)} %broadcast.1574), channel_id=1, source_target_pairs={{0,4},{4,8},{8,12},{12,16},{16,20},{20,24},{24,28},{28,32},{32,36}... | collective-permute-start | bytes 1544 | tf_op jit(solution)/shard_map/ppermute | solution.py:25
  66.1 5.5 collective-permute-start.17
  66.2 5.7 collective-permute-start.16
  72.0 4.0 collective-permute-start.19
  72.1 4.0 collective-permute-start.18
  79.4 7.2 collective-permute-start.21
  79.5 7.3 collective-permute-start.20
  86.9 4.3 collective-permute-start.23
  87.3 3.9 collective-permute-start.22
  92.7 7.0 collective-permute-start.25
  98.9 4.8 collective-permute-start.24
  112.0 8.8 collective-permute-start.33
  286.7 3.9 collective-permute-start.38
  452.3 3.8 collective-permute-start.42
  721.2 4.3 collective-permute-start.55
  721.6 3.8 collective-permute-start.54
  728.6 6.4 collective-permute-start.57
  729.3 5.9 collective-permute-start.56
  735.3 4.6 collective-permute-start.59
  741.3 7.1 collective-permute-start.61
  747.7 4.8 collective-permute-start.60
  760.4 8.0 collective-permute-start.65
  768.9 4.4 collective-permute-start.66
  1369.8 4.3 collective-permute-start.87
  1370.2 3.8 collective-permute-start.86
  1377.2 6.4 collective-permute-start.89
  1377.9 5.9 collective-permute-start.88
  1383.9 4.4 collective-permute-start.91
  1389.7 7.6 collective-permute-start.93
  1396.5 4.6 collective-permute-start.92
  1409.2 8.0 collective-permute-start.97
  1417.6 4.0 collective-permute-start.98
  (127 other events, 1948.4 us)
where the time goes:
time: 2030 us; the launch traced here: 2010 us
  blocking collectives  1580 us (78%)
  starting transfers between devices  192 us (9%)
  waiting for transfers between devices  118 us (6%)
  matrix products  39.1 us (2%)
  between operations  31.9 us (2%)
  local copies, waits for them, and re-layouts  25.3 us (1%)
  other arithmetic  22.3 us (1%)
    psum x21, blocking collectives, coarse_inner(): lax.psum(jnp.sum(left_side * right_part / coarse_count), ('elem', 'sub'))  1580 us
    ppermute x58, starting transfers between devices, extended(): lax.ppermute(lax.slice_in_dim(block, 0, width, axis=dim), axis, backward)  149 us
    ppermute x58, waiting for transfers between devices, extended(): lax.ppermute(lax.slice_in_dim(block, block.shape[dim] - width, None, axis...  78.7 us
    ppermute x58, starting transfers between devices, extended(): lax.ppermute(lax.slice_in_dim(block, block.shape[dim] - width, None, axis...  42.5 us
  transfers between devices with their start and end apart: 116, of which 95 were waited for; matrix products, arithmetic and copies ran while one was open for 1% of the time, Pallas kernels for 0%

commit v1 on v0

v1 whole, which is shorter than its diff:
```python
import functools

import jax
import jax.numpy as jnp
import ml_dtypes
import numpy as np
from jax import lax
from jax.experimental import pallas as pl
from jax.experimental.pallas import tpu as pltpu
from jax.sharding import PartitionSpec as P

POINTS = 8
SUBSTEPS = 3
MG_ITERS = 3
COARSE_ITERS = 4

TIME_STEP = 0.005
SHIFT_COEF = 0.05
RELAXATION = 0.6
SOURCE_GAIN = 20.0

MESH = pl.DeviceIdType.MESH
ROUNDS = SUBSTEPS + 2 * MG_ITERS


def legendre_last(points, degree):
    previous = points * 0.0 + 1.0
    current = points + 0.0
    for level in range(2, degree + 1):
        following = ((2 * level - 1) * points * current - (level - 1) * previous) / level
        previous = current
        current = following
    return (previous, current)


def gll_tables(count):
    degree = count - 1
    points = -np.cos(np.pi * np.arange(count) / degree)
    for sweep in range(100):
        before_last, last_value = legendre_last(points, degree)
        points = points - (points * last_value - before_last) / (count * last_value)
    before_last, legendre = legendre_last(points, degree)
    weights = 2.0 / (degree * (degree + 1) * legendre**2)
    spacing = points[:, None] - points[None, :] + np.eye(count)
    matrix = legendre[:, None] / (legendre[None, :] * spacing) * (1.0 - np.eye(count))
    matrix[0, 0] = -degree * (degree + 1) / 4.0
    matrix[degree, degree] = degree * (degree + 1) / 4.0
    return (points, weights, matrix)


def assembled(values, walls):
    blocks = values.reshape(-1, POINTS)
    out = blocks.copy()
    out[:, 0] += blocks[:, -1]
    out[:, -1] += blocks[:, 0]
    if walls:
        out[0, 0] = blocks[0, 0]
        out[-1, -1] = blocks[-1, -1]
    return out.reshape(-1)


def coarse_tables(elements, lift, stiff, walls):
    count = elements * POINTS
    vertices = elements + 1
    interp = np.zeros((count, vertices + 2))
    slope = np.zeros((count, vertices + 2))
    edge = stiff @ lift
    for element in range(elements):
        for point in range(POINTS):
            row = element * POINTS + point
            pairs = [(element, point)]
            if point == 0 and not (walls and element == 0):
                pairs.append((element - 1, POINTS - 1))
            if point == POINTS - 1 and not (walls and element == elements - 1):
                pairs.append((element + 1, 0))
            for side in (0, 1):
                interp[row, element + side + 1] += lift[point, side]
                for other, at in pairs:
                    slope[row, other + side + 1] += edge[at, side]
    slope[np.abs(slope) < 1e-12] = 0.0
    return (interp[:, 1:-1], slope[:, 1:-1]) if walls else (interp, slope)


def halves(matrix):
    whole = np.asarray(matrix, np.float32)
    high = whole.astype(ml_dtypes.bfloat16)
    low = (whole - high.astype(np.float32)).astype(ml_dtypes.bfloat16)
    return np.stack([high, low])


def make_tables():
    points, weights, deriv = gll_tables(POINTS)
    stiff = deriv.T @ np.diag(weights) @ deriv
    scaled = np.diag(1.0 / weights) @ stiff
    squares = (deriv * deriv).T @ weights
    lift = np.stack([(1.0 - points) / 2.0, (1.0 + points) / 2.0], axis=1)
    kron, eye = np.kron, np.eye
    wz, wx, wy = weights, np.tile(weights, 2), np.tile(weights, 16)
    waz, wax, way = assembled(wz, False), assembled(wx, False), assembled(wy, True)
    saz = assembled(squares, False)
    sax = assembled(np.tile(squares, 2), False)
    say = assembled(np.tile(squares, 16), True)

    def outer(a, b, c):
        return kron(a, b)[:, None] * c[None, :]

    local = outer(wz, wx, wy) / 8.0
    mass = outer(waz, wax, way) / 8.0
    diagonal = 0.5 * (outer(saz, wax, way) + outer(waz, sax, way) + outer(waz, wax, say))
    diagonal = diagonal + SHIFT_COEF * mass
    jz, kz = coarse_tables(1, lift, stiff, False)
    jx, kx = coarse_tables(2, lift, stiff, False)
    jy, ky = coarse_tables(16, lift, stiff, True)

    def lanes(table):
        out = np.zeros((table.shape[0], 128))
        out[:, :68] = np.tile(table, (1, 4))
        return out

    left = kron(scaled, eye(16)) + kron(eye(8), kron(eye(2), scaled)) + SHIFT_COEF / 4.0 * eye(128)
    matrices = [
        kron(deriv, eye(16)),
        kron(eye(8), kron(eye(2), deriv)),
        kron(eye(16), deriv).T,
        left,
        kron(eye(16), scaled).T,
        lanes(way[:, None] * jy),
        lanes(ky),
        lanes(jy),
        lanes(jy).T,
        lanes(ky).T,
    ]
    matrices = np.stack([halves(one) for one in matrices])
    fields = np.stack(
        [
            4.0 * local,
            local / mass,
            RELAXATION / diagonal,
            0.5 * outer(waz, wax, np.ones(128)),
        ]
    ).astype(np.float32)
    lane = np.arange(128)
    inner = lane % POINTS
    level = lane % 17
    valid = lane < 68
    rows = np.zeros((8, 128), np.float32)
    rows[0] = (inner == 0) & (lane > 0)
    rows[1] = (inner == POINTS - 1) & (lane < 127)
    rows[2] = way
    rows[3] = np.where(valid, np.where((level == 0) | (level == 16), 1.0, 2.0), 0.0)
    rows[4] = valid & (level < 16)
    rows[5] = valid & (level > 0)
    kinds = [jx, wax[:, None] * jx, 0.5 * kx + SHIFT_COEF / 8.0 * wax[:, None] * jx]
    spans = np.zeros((4, 6, 16, 128), np.float32)
    for sub in range(4):
        for kind, table in enumerate(kinds):
            for half in range(2):
                for slot in range(4):
                    column = (2 * slot + half - 2 * sub + 1) % 8
                    if column < 5:
                        spans[sub, kind * 2 + half, :, slot * 17 : slot * 17 + 17] = table[
                            :, column : column + 1
                        ]
    return matrices, fields, rows, spans, jz, kz, waz


M_DZ, M_DX, M_DY, M_LEFT, M_RIGHT, M_JYW, M_KY, M_JY, M_JYT, M_KYT = range(10)


def kernel(
    zcoef,
    count,
    vel_in,
    mats,
    fields,
    rows,
    spans,
    adv_out,
    p_out,
    vel,
    sloc,
    pres,
    csrc,
    work,
    acc,
    xs,
    co,
    zr,
    xr,
    cr,
    g1,
    g2,
    ext,
    n_send,
    n_recv,
    a_send,
    a_recv,
    b_send,
    b_recv,
):
    jz, kz, waz = zcoef
    blocks = count // 4
    tiles = blocks // 2
    elem = lax.axis_index("elem")
    sub = lax.axis_index("sub")
    block = elem // 4
    place = elem % 4
    slot = place * 4 + sub

    def near(de, ds):
        return (lax.rem(elem + de + count, count), lax.rem(sub + ds + 4, 4))

    near_ids = [
        near(1, 1),
        near(1, -1),
        near(-1, 1),
        near(-1, -1),
        near(1, 0),
        near(-1, 0),
        near(0, 1),
        near(0, -1),
    ]
    a_ids = [
        (block * 4 + lax.rem(place + dj, 4), lax.rem(sub + ds, 4))
        for dj in range(4)
        for ds in range(4)
        if dj or ds
    ]
    b_ids = [(lax.rem(block + db, blocks) * 4 + place, sub) for db in range(1, blocks)]

    barrier = pltpu.get_barrier_semaphore()
    partners = near_ids + a_ids + b_ids
    for one in partners:
        pl.semaphore_signal(barrier, inc=1, device_id=one, device_id_type=MESH)

    sublane = lax.broadcasted_iota(jnp.int32, (8, 128), 0)
    low_lane, high_lane = rows[0:1, :], rows[1:2, :]

    def split(x):
        high = x.astype(jnp.bfloat16)
        return high, (x - high.astype(jnp.float32)).astype(jnp.bfloat16)

    def mul(a, b):
        return jnp.dot(a, b, preferred_element_type=jnp.float32)

    def left_dot(index, parts):
        high, low = parts
        return mul(mats[index, 0], high) + (mul(mats[index, 0], low) + mul(mats[index, 1], high))

    def right_dot(parts, index):
        high, low = parts
        return mul(high, mats[index, 0]) + (mul(low, mats[index, 0]) + mul(high, mats[index, 1]))

    def near_copies(r, comps):
        pairs = [
            (co.at[r, 0], cr.at[r, 0]),
            (co.at[r, 1], cr.at[r, 1]),
            (co.at[r, 2], cr.at[r, 2]),
            (co.at[r, 3], cr.at[r, 3]),
            (work.at[r, pl.ds(0, comps), pl.ds(112, 16)], zr.at[r, 0, pl.ds(0, comps)]),
            (work.at[r, pl.ds(0, comps), pl.ds(0, 16)], zr.at[r, 1, pl.ds(0, comps)]),
            (xs.at[r, 1, pl.ds(0, comps)], xr.at[r, 0, pl.ds(0, comps)]),
            (xs.at[r, 0, pl.ds(0, comps)], xr.at[r, 1, pl.ds(0, comps)]),
        ]
        return [
            pltpu.make_async_remote_copy(
                src_ref=src,
                dst_ref=dst,
                send_sem=n_send.at[r, k],
                recv_sem=n_recv.at[r, k],
                device_id=near_ids[k],
                device_id_type=MESH,
            )
            for k, (src, dst) in enumerate(pairs)
        ]

    def start_near(r, comps):
        for corner, row in enumerate((127, 112, 15, 0)):
            tile = jnp.zeros((8, 128), jnp.float32)
            for c in range(comps):
                tile = jnp.where(sublane == c, work[r, c, row : row + 1, :], tile)
            co[r, corner] = tile
        for c in range(comps):
            xs[r, 0, c] = work[r, c, pl.ds(0, 8, stride=16), :]
            xs[r, 1, c] = work[r, c, pl.ds(15, 8, stride=16), :]
        for copy in near_copies(r, comps):
            copy.start()

    def finish_near(r, comps):
        for copy in near_copies(r, comps):
            copy.wait_recv()
        out = []
        for c in range(comps):
            acc[c, 0:16] = work[r, c, 0:16] + zr[r, 0, c]
            acc[c, 16:112] = work[r, c, 16:112]
            acc[c, 112:128] = work[r, c, 112:128] + zr[r, 1, c]
            both = acc[c, pl.ds(7, 8, stride=16), :] + acc[c, pl.ds(8, 8, stride=16), :]
            acc[c, pl.ds(7, 8, stride=16), :] = both
            acc[c, pl.ds(8, 8, stride=16), :] = both
            for side, row in ((0, 0), (1, 15)):
                face = xr[r, side, c]
                face = face + jnp.where(sublane == 0, cr[r, side, c : c + 1, :], 0.0)
                face = face + jnp.where(sublane == 7, cr[r, 2 + side, c : c + 1, :], 0.0)
                acc[c, pl.ds(row, 8, stride=16), :] = acc[c, pl.ds(row, 8, stride=16), :] + face
            field = acc[c]
            field = (
                field
                + low_lane * pltpu.roll(field, 1, 1)
                + high_lane * pltpu.roll(field, 127, 1)
            )
            out.append(field)
        return out

    for c in range(3):
        vel[c] = vel_in[c].reshape(128, 128)
    pl.semaphore_wait(barrier, len(partners))

    def substep(i, carry):
        parts = [split(vel[c]) for c in range(3)]
        for c in range(3):
            term = vel[0] * left_dot(M_DZ, parts[c])
            term = term + vel[1] * left_dot(M_DX, parts[c])
            term = term + vel[2] * right_dot(parts[c], M_DY)
            work[i, c] = term * ((2.0 * TIME_STEP) * fields[1])
        start_near(i, 3)
        shared = finish_near(i, 3)
        for c in range(3):
            vel[c] = vel[c] - shared[c]
        return carry

    lax.fori_loop(0, SUBSTEPS, substep, 0)

    for c in range(3):
        adv_out[c] = vel[c].reshape(8, 16, 128)
    divergence = left_dot(M_DZ, split(vel[0])) + left_dot(M_DX, split(vel[1]))
    divergence = divergence + right_dot(split(vel[2]), M_DY)
    source = (-SOURCE_GAIN / 4.0) * fields[0] * divergence
    sloc[...] = source
    pres[...] = jnp.zeros_like(source)
    direct = right_dot(split(source), M_JY).reshape(8, 16, 128)
    for half in range(2):
        span = spans[sub, half]
        for zi in range(4):
            total = None
            for z in range(8):
                if jz[z, zi] != 0.0:
                    one = float(jz[z, zi]) * direct[z]
                    total = one if total is None else total + one
            if total is None:
                row = jnp.zeros((1, 128), jnp.float32)
            else:
                row = jnp.sum(total * span, axis=0, keepdims=True)
            csrc[half * 4 + zi : half * 4 + zi + 1, :] = row

    def weighted(table, zi, field):
        total = None
        for z in range(8):
            if table[z, zi] != 0.0:
                one = float(table[z, zi]) * field[z]
                total = one if total is None else total + one
        return total

    wjz = waz[:, None] * jz

    def minus_laplace(field):
        parts = split(field)
        return sloc[...] - fields[0] * (left_dot(M_LEFT, parts) + right_dot(parts, M_RIGHT))

    def a_copies(it):
        return [
            pltpu.make_async_remote_copy(
                src_ref=g1.at[it, slot],
                dst_ref=g1.at[it, slot],
                send_sem=a_send.at[it, k],
                recv_sem=a_recv.at[it, k],
                device_id=one,
                device_id_type=MESH,
            )
            for k, one in enumerate(a_ids)
        ]

    def b_copies(it):
        return [
            pltpu.make_async_remote_copy(
                src_ref=g2.at[it, block],
                dst_ref=g2.at[it, block],
                send_sem=b_send.at[it, k],
                recv_sem=b_recv.at[it, k],
                device_id=one,
                device_id_type=MESH,
            )
            for k, one in enumerate(b_ids)
        ]

    def coarse_apply(pair):
        my, up, down = rows[3:4, :], rows[4:5, :], rows[5:6, :]
        even, odd = pair
        across = (
            odd + pltpu.roll(odd, 17, 1) + pltpu.roll(odd, 77, 1),
            even + pltpu.roll(even, 111, 1) + pltpu.roll(even, 51, 1),
        )
        out = []
        for u, near_x in zip(pair, across):
            near_z = pltpu.roll(u, 1, 0) + pltpu.roll(u, u.shape[0] - 1, 0)
            one = my * (3.025 * u - 0.5 * (near_z + near_x))
            out.append(one - up * pltpu.roll(u, 127, 1) - down * pltpu.roll(u, 1, 1))
        return out

    def inner(a, b):
        return jnp.sum(a[0] * b[0] + a[1] * b[1], keepdims=True)

    def conjugate(right_side):
        solution = None
        residual = right_side
        direction = right_side
        norm_now = inner(residual, residual)
        for sweep in range(COARSE_ITERS):
            image = coarse_apply(direction)
            alpha = norm_now / inner(direction, image)
            step = [alpha * d for d in direction]
            solution = step if solution is None else [x + d for x, d in zip(solution, step)]
            if sweep == COARSE_ITERS - 1:
                break
            residual = [x - alpha * d for x, d in zip(residual, image)]
            norm_next = inner(residual, residual)
            beta = norm_next / norm_now
            direction = [x + beta * d for x, d in zip(residual, direction)]
            norm_now = norm_next
        return solution

    def cycle(it, carry):
        first = SUBSTEPS + 2 * it
        second = first + 1
        pressure = pres[...]
        local = minus_laplace(pressure)
        work[first, 0] = local
        mixed = split(pressure * fields[1] + fields[2] * local)
        flat = right_dot(mixed, M_JYW).reshape(8, 16, 128)
        bent = right_dot(mixed, M_KY).reshape(8, 16, 128)
        for zi in range(4):
            edge = 0.5 * weighted(kz, zi, flat)
            body = weighted(wjz, zi, flat)
            if body is not None:
                edge = edge + 0.5 * weighted(wjz, zi, bent)
            for half in range(2):
                total = edge * spans[sub, 2 + half]
                if body is not None:
                    total = total + body * spans[sub, 4 + half]
                at = half * 4 + zi
                row = jnp.sum(total, axis=0, keepdims=True)
                g1[it, slot, at : at + 1, :] = csrc[at : at + 1, :] - row
        for copy in a_copies(it):
            copy.start()
        start_near(first, 1)

        for copy in a_copies(it):
            copy.wait_recv()
        tops = []
        for j in range(4):
            tops.append(g1[it, 4 * j] + g1[it, 4 * j + 1] + (g1[it, 4 * j + 2] + g1[it, 4 * j + 3]))
        odd_block = lax.rem(block, 2) == 1
        for half in range(2):
            total = None
            for j in range(4):
                shift = (j - 4 * half) % 8
                moved = pltpu.roll(tops[j], shift, 0) if shift else tops[j]
                moved = jnp.where((sublane >= j) & (sublane < j + 4), moved, 0.0)
                total = moved if total is None else total + moved
            total = jnp.where(odd_block, pltpu.roll(total, 3, 0), pltpu.roll(total, 7, 0))
            g2[it, block, half * 8 : half * 8 + 8, :] = total
        for copy in b_copies(it):
            copy.start()

        shared = finish_near(first, 1)[0]
        pressure = pressure + fields[2] * shared
        pres[...] = pressure
        work[second, 0] = minus_laplace(pressure)
        start_near(second, 1)

        for copy in b_copies(it):
            copy.wait_recv()
        right_side = []
        for half in range(2):
            at = slice(half * 8, half * 8 + 8)
            pieces = []
            for t in range(tiles):
                one = jnp.where(sublane < 6, g2[it, 2 * t, at, :], 0.0)
                one = one + jnp.where(sublane >= 3, g2[it, 2 * t + 1, at, :], 0.0)
                one = one + jnp.where(sublane == 7, g2[it, (2 * t + 2) % blocks, at, :], 0.0)
                one = one + jnp.where(sublane < 2, g2[it, (2 * t - 1) % blocks, at, :], 0.0)
                pieces.append(one)
            right_side.append(jnp.concatenate(pieces, axis=0))
        answer = conjugate(right_side)
        vertex = []
        for half in range(2):
            ext[half, 0:8] = answer[half][count - 8 : count]
            ext[half, 8 : 8 + count] = answer[half]
            ext[half, 8 + count : 16 + count] = answer[half][0:8]
            vertex.append([ext[half, pl.ds(elem + 7 + v, 1), :] for v in range(4)])

        interp, image = [], []
        for z in range(8):
            one, two = None, None
            for half in range(2):
                value = float(jz[z, 1]) * vertex[half][1] + float(jz[z, 2]) * vertex[half][2]
                part = value * spans[sub, half]
                one = part if one is None else one + part
                part = (float(waz[z]) * value) * spans[sub, 4 + half]
                if np.any(kz[z] != 0.0):
                    bend = None
                    for v in range(4):
                        if kz[z, v] != 0.0:
                            term = (0.5 * float(kz[z, v])) * vertex[half][v]
                            bend = term if bend is None else bend + term
                    part = part + bend * spans[sub, 2 + half]
                two = part if two is None else two + part
            interp.append(one)
            image.append(two)
        interp = split(jnp.concatenate(interp, axis=0))
        image = split(jnp.concatenate(image, axis=0))
        correction = right_dot(interp, M_JYT)
        applied = rows[2:3, :] * right_dot(image, M_JYT)
        applied = applied + fields[3] * right_dot(interp, M_KYT)
        shared = finish_near(second, 1)[0]
        pres[...] = pres[...] + correction + fields[2] * (shared - applied)
        return carry

    lax.fori_loop(0, MG_ITERS, cycle, 0)
    p_out[...] = pres[...].reshape(8, 16, 128)

    def drain_substep(i, carry):
        for copy in near_copies(i, 3):
            copy.wait_send()
        return carry

    lax.fori_loop(0, SUBSTEPS, drain_substep, 0)

    def drain_cycle(it, carry):
        for r in (SUBSTEPS + 2 * it, SUBSTEPS + 2 * it + 1):
            for copy in near_copies(r, 1):
                copy.wait_send()
        for copy in a_copies(it) + b_copies(it):
            copy.wait_send()
        return carry

    lax.fori_loop(0, MG_ITERS, drain_cycle, 0)


def solution(mesh):
    count = mesh.shape["elem"]
    matrices, fields, rows, spans, jz, kz, waz = make_tables()
    blocks = count // 4
    f32 = jnp.float32

    def shards(velocity):
        vmem = pl.BlockSpec(memory_space=pltpu.VMEM)
        return pl.pallas_call(
            functools.partial(kernel, (jz, kz, waz), count),
            out_shape=(
                jax.ShapeDtypeStruct((3, 8, 16, 128), f32),
                jax.ShapeDtypeStruct((8, 16, 128), f32),
            ),
            in_specs=[vmem] * 5,
            out_specs=(vmem, vmem),
            scratch_shapes=[
                pltpu.VMEM((3, 128, 128), f32),
                pltpu.VMEM((128, 128), f32),
                pltpu.VMEM((128, 128), f32),
                pltpu.VMEM((8, 128), f32),
                pltpu.VMEM((ROUNDS, 3, 128, 128), f32),
                pltpu.VMEM((3, 128, 128), f32),
                pltpu.VMEM((ROUNDS, 2, 3, 8, 128), f32),
                pltpu.VMEM((ROUNDS, 4, 8, 128), f32),
                pltpu.VMEM((ROUNDS, 2, 3, 16, 128), f32),
                pltpu.VMEM((ROUNDS, 2, 3, 8, 128), f32),
                pltpu.VMEM((ROUNDS, 4, 8, 128), f32),
                pltpu.VMEM((MG_ITERS, 16, 8, 128), f32),
                pltpu.VMEM((MG_ITERS, blocks, 16, 128), f32),
                pltpu.VMEM((2, count + 16, 128), f32),
                pltpu.SemaphoreType.DMA((ROUNDS, 8)),
                pltpu.SemaphoreType.DMA((ROUNDS, 8)),
                pltpu.SemaphoreType.DMA((MG_ITERS, 15)),
                pltpu.SemaphoreType.DMA((MG_ITERS, 15)),
                pltpu.SemaphoreType.DMA((MG_ITERS, blocks - 1)),
                pltpu.SemaphoreType.DMA((MG_ITERS, blocks - 1)),
            ],
            compiler_params=pltpu.CompilerParams(
                collective_id=0, has_side_effects=True, vmem_limit_bytes=32 * 1024 * 1024
            ),
        )(
            velocity,
            jnp.asarray(matrices),
            jnp.asarray(fields),
            jnp.asarray(rows),
            jnp.asarray(spans),
        )

    return jax.shard_map(
        shards,
        mesh=mesh,
        in_specs=(P(None, "elem", "sub", None),),
        out_specs=(P(None, "elem", "sub", None), P("elem", "sub", None)),
        check_vma=False,
    )
```

time: 2030 us -> 76.2 us (0.04)
  blocking collectives: 1580 us -> 0 us
  starting transfers between devices: 192 us -> 0 us
  waiting for transfers between devices: 118 us -> 0 us
  Pallas kernels: 0 us -> 69.4 us
  matrix products: 39.1 us -> 0 us
  between operations: 31.9 us -> 0.65 us
  other arithmetic: 22.3 us -> 0 us
    psum x21 -> x0, blocking collectives: 1580 us -> none  [coarse_inner(): lax.psum(jnp.sum(left_side * right_part / coarse_count), ('elem', 'sub'))]
    ppermute x116 -> x0, starting transfers between devices: 192 us -> none  [the longest x58 149 us: extended(): lax.ppermute(lax.slice_in_dim(block, 0, width, axis=dim), axis, backward)]
    ppermute x116 -> x0, waiting for transfers between devices: 118 us -> none  [the longest x58 78.7 us: extended(): lax.ppermute(lax.slice_in_dim(block, block.shape[dim] - width, None, axis...]
    pallas_call x0 -> x1, Pallas kernels: none -> 69.4 us  [shards(): pl.pallas_call(functools.partial(kernel, (jz, kz, waz), count), out_shape...]
    dot_general x150 -> x0, matrix products: 39.1 us -> none  [apply_axis(): jnp.einsum(forms[axis], table, field.reshape(split), precision=lax.Precis...]
  transfers between devices with their start and end apart: 116 -> 0, of which waited for: 95 -> 0; matrix products, arithmetic and copies ran while one was open for 1% -> 0% of each run, Pallas kernels for 0% -> 0%
where the time goes in v1:
time: 76.2 us; the launch traced here: 75.9 us
  Pallas kernels  69.4 us (91%)
  local copies, waits for them, and re-layouts  5.88 us (8%)
    pallas_call x1, Pallas kernels, shards(): pl.pallas_call(functools.partial(kernel, (jz, kz, waz), count), out_shape...  69.4 us
    unnamed x12, local copies, waits for them, and re-layouts  5.88 us

profile of v1, /device:TPU:1, one launch (start us, length us, event | category | flops | bytes accessed | tf_op | source)
XLA Modules:
  0.0 75.9 jit_solution(7269565443683584358)
XLA Ops:
  0.6 0.0 copy-start
  0.6 1.1 %copy-done = bf16[10,2,128,128]{3,2,1,0:T(8,128)(2,1)S(1)} copy-done((bf16[10,2,128,128]{3,2,1,0:T(8,128)(2,1)S(1)}, bf16[10,2,128,128]{3,2,1,0:T(8,128)(2,1)}, u32[]{:S(2)}) %copy-start) | copy-done | bytes 655384
  1.7 0.0 copy-start.1
  1.7 0.9 %copy-done.1 = f32[4,128,128]{2,1,0:T(8,128)S(1)} copy-done((f32[4,128,128]{2,1,0:T(8,128)S(1)}, f32[4,128,128]{2,1,0:T(8,128)}, u32[]{:S(2)}) %copy-start.1) | copy-done | bytes 262168
  2.7 0.0 copy-start.2
  2.7 0.9 %copy-done.2 = f32[3,8,16,128]{3,2,1,0:T(8,128)S(1)} copy-done((f32[3,8,16,128]{3,2,1,0:T(8,128)S(1)}, f32[3,8,16,128]{3,2,1,0:T(8,128)}, u32[]{:S(2)}) %copy-start.2) | copy-done | bytes 196632
  3.6 0.0 copy-start.3
  3.6 0.9 %copy-done.3 = f32[4,6,16,128]{3,2,1,0:T(8,128)S(1)} copy-done((f32[4,6,16,128]{3,2,1,0:T(8,128)S(1)}, f32[4,6,16,128]{3,2,1,0:T(8,128)}, u32[]{:S(2)}) %copy-start.3) | copy-done | bytes 196632
  4.5 0.0 copy-start.4
  4.5 0.7 copy-done.4
  5.2 69.4 %shard_map.68 = (f32[3,8,16,128]{3,2,1,0:T(8,128)S(1)}, f32[8,16,128]{2,1,0:T(8,128)S(1)}) custom-call(f32[3,8,16,128]{3,2,1,0:T(8,128)S(1)} %copy-done.2, bf16[10,2,128,128]{3,2,1,0:T(8,128)(2,1)S(1)} %copy-done, f32[4,128,128]{2,1,0:T(8,128)S(1)} %copy-done.1, f32[8,128]{1,0:T(8,128)S(1)} %copy-done.4, f32[4,6,16,128]{3,2,1,0:T(8,128)S(1)} %copy-done.3), custom_call_target="tpu_custom_call" | custom-call | tf_op jit(solution)/shard_map/pallas_call | solution.py:557
  74.6 0.7 copy.9
  75.3 0.6 copy.10
Async XLA Ops:
  0.6 1.1 %copy-start = (bf16[10,2,128,128]{3,2,1,0:T(8,128)(2,1)S(1)}, bf16[10,2,128,128]{3,2,1,0:T(8,128)(2,1)}, u32[]{:S(2)}) copy-start(bf16[10,2,128,128]{3,2,1,0:T(8,128)(2,1)} %constant.8.clone.mats) | copy-start | bytes 1966084
  1.7 0.9 %copy-start.1 = (f32[4,128,128]{2,1,0:T(8,128)S(1)}, f32[4,128,128]{2,1,0:T(8,128)}, u32[]{:S(2)}) copy-start(f32[4,128,128]{2,1,0:T(8,128)} %constant.9.clone.fields) | copy-start | bytes 786436
  2.7 0.9 %copy-start.2 = (f32[3,8,16,128]{3,2,1,0:T(8,128)S(1)}, f32[3,8,16,128]{3,2,1,0:T(8,128)}, u32[]{:S(2)}) copy-start(f32[3,8,16,128]{3,2,1,0:T(8,128)} %vel_in.1) | copy-start | bytes 589828
  3.6 0.9 %copy-start.3 = (f32[4,6,16,128]{3,2,1,0:T(8,128)S(1)}, f32[4,6,16,128]{3,2,1,0:T(8,128)}, u32[]{:S(2)}) copy-start(f32[4,6,16,128]{3,2,1,0:T(8,128)} %constant.11.clone.spans) | copy-start | bytes 589828
  4.5 0.7 copy-start.4

commit v2 on v1

--- a/solution.py
+++ b/solution.py
@@ -171,13 +171,17 @@
     zcoef,
     count,
     vel_in,
+    mats_in,
+    fields_in,
+    rows_in,
+    spans_in,
+    adv_out,
+    p_out,
+    vel,
     mats,
     fields,
     rows,
     spans,
-    adv_out,
-    p_out,
-    vel,
     sloc,
     pres,
     csrc,
@@ -191,12 +195,16 @@
     g1,
     g2,
     ext,
+    gauge,
+    load,
     n_send,
     n_recv,
     a_send,
     a_recv,
     b_send,
     b_recv,
+    known_side,
+    known_row,
 ):
     jz, kz, waz = zcoef
     blocks = count // 4
@@ -209,6 +217,11 @@
 
     def near(de, ds):
         return (lax.rem(elem + de + count, count), lax.rem(sub + ds + 4, 4))
+
+    def at_block(dx, dz):
+        bx, bz = block // 4, block % 4
+        other = lax.rem(bx + dx, blocks // 4) * 4 + lax.rem(bz + dz, 4)
+        return (other * 4 + place, sub)
 
     near_ids = [
         near(1, 1),
@@ -222,19 +235,36 @@
     ]
     a_ids = [
         (block * 4 + lax.rem(place + dj, 4), lax.rem(sub + ds, 4))
-        for dj in range(4)
-        for ds in range(4)
+        for ds in (2, 1, 3, 0)
+        for dj in (2, 1, 3, 0)
         if dj or ds
     ]
-    b_ids = [(lax.rem(block + db, blocks) * 4 + place, sub) for db in range(1, blocks)]
-
+    b_ids = [
+        at_block(dx, dz)
+        for dz in (2, 1, 3, 0)
+        for dx in (2, 1, 3, 0)
+        if (dx or dz) and dx < blocks // 4
+    ]
+    row_ids = [at_block(dx, 0) for dx in range(1, blocks // 4)]
+    side_ids = [at_block(0, 1), at_block(0, 3)]
+
+    loads = [
+        pltpu.make_async_copy(src, dst, load.at[k])
+        for k, (src, dst) in enumerate(
+            ((vel_in, vel), (mats_in, mats), (fields_in, fields), (rows_in, rows), (spans_in, spans))
+        )
+    ]
+    for copy in loads:
+        copy.start()
     barrier = pltpu.get_barrier_semaphore()
-    partners = near_ids + a_ids + b_ids
+    partners = near_ids + side_ids + row_ids
     for one in partners:
         pl.semaphore_signal(barrier, inc=1, device_id=one, device_id_type=MESH)
 
     sublane = lax.broadcasted_iota(jnp.int32, (8, 128), 0)
-    low_lane, high_lane = rows[0:1, :], rows[1:2, :]
+    lane = lax.broadcasted_iota(jnp.int32, (1, 128), 1)
+    low_lane = jnp.where((lane % 8 == 0) & (lane > 0), 1.0, 0.0)
+    high_lane = jnp.where((lane % 8 == 7) & (lane < 127), 1.0, 0.0)
 
     def split(x):
         high = x.astype(jnp.bfloat16)
@@ -266,13 +296,20 @@
             pltpu.make_async_remote_copy(
                 src_ref=src,
                 dst_ref=dst,
-                send_sem=n_send.at[r, k],
-                recv_sem=n_recv.at[r, k],
+                send_sem=n_send.at[r],
+                recv_sem=n_recv.at[r],
                 device_id=near_ids[k],
                 device_id_type=MESH,
             )
             for k, (src, dst) in enumerate(pairs)
         ]
+
+    def take(sem, count_rows):
+        part = gauge.at[pl.ds(0, count_rows)]
+        pltpu.make_async_copy(part, part, sem).wait()
+
+    def near_rows(comps):
+        return 32 + 48 * comps
 
     def start_near(r, comps):
         for corner, row in enumerate((127, 112, 15, 0)):
@@ -286,52 +323,77 @@
         for copy in near_copies(r, comps):
             copy.start()
 
+    def share_y(field):
+        return (
+            field
+            + low_lane * pltpu.roll(field, 1, 1)
+            + high_lane * pltpu.roll(field, 127, 1)
+        )
+
     def finish_near(r, comps):
-        for copy in near_copies(r, comps):
-            copy.wait_recv()
-        out = []
         for c in range(comps):
-            acc[c, 0:16] = work[r, c, 0:16] + zr[r, 0, c]
-            acc[c, 16:112] = work[r, c, 16:112]
-            acc[c, 112:128] = work[r, c, 112:128] + zr[r, 1, c]
+            acc[c] = share_y(work[r, c])
             both = acc[c, pl.ds(7, 8, stride=16), :] + acc[c, pl.ds(8, 8, stride=16), :]
             acc[c, pl.ds(7, 8, stride=16), :] = both
             acc[c, pl.ds(8, 8, stride=16), :] = both
+        take(n_recv.at[r], near_rows(comps))
+        for c in range(comps):
+            for side, row in ((0, 0), (1, 112)):
+                first = zr[r, side, c, 0:8]
+                second = zr[r, side, c, 8:16]
+                both = share_y(first + jnp.where(sublane == 7, pltpu.roll(second, 7, 0), 0.0))
+                acc[c, row : row + 8] = acc[c, row : row + 8] + both
+                both = share_y(second + jnp.where(sublane == 0, pltpu.roll(first, 1, 0), 0.0))
+                acc[c, row + 8 : row + 16] = acc[c, row + 8 : row + 16] + both
             for side, row in ((0, 0), (1, 15)):
                 face = xr[r, side, c]
                 face = face + jnp.where(sublane == 0, cr[r, side, c : c + 1, :], 0.0)
                 face = face + jnp.where(sublane == 7, cr[r, 2 + side, c : c + 1, :], 0.0)
-                acc[c, pl.ds(row, 8, stride=16), :] = acc[c, pl.ds(row, 8, stride=16), :] + face
-            field = acc[c]
-            field = (
-                field
-                + low_lane * pltpu.roll(field, 1, 1)
-                + high_lane * pltpu.roll(field, 127, 1)
-            )
-            out.append(field)
-        return out
-
-    for c in range(3):
-        vel[c] = vel_in[c].reshape(128, 128)
-    pl.semaphore_wait(barrier, len(partners))
-
-    def substep(i, carry):
+                acc[c, pl.ds(row, 8, stride=16), :] = acc[c, pl.ds(row, 8, stride=16), :] + share_y(face)
+
+    def advect(i):
         parts = [split(vel[c]) for c in range(3)]
         for c in range(3):
             term = vel[0] * left_dot(M_DZ, parts[c])
             term = term + vel[1] * left_dot(M_DX, parts[c])
             term = term + vel[2] * right_dot(parts[c], M_DY)
             work[i, c] = term * ((2.0 * TIME_STEP) * fields[1])
+
+    for copy in loads:
+        copy.wait()
+    advect(0)
+    pl.semaphore_wait(barrier, len(partners))
+
+    def pass_on(known, ids):
+        for one in ids:
+            pl.semaphore_signal(known, inc=1, device_id=one, device_id_type=MESH)
+        pl.semaphore_wait(known, len(ids))
+
+    def substep(i, carry):
         start_near(i, 3)
-        shared = finish_near(i, 3)
+
+        @pl.when(i == 0)
+        def _():
+            pass_on(known_side, side_ids)
+
+        @pl.when(i == 1)
+        def _():
+            pass_on(known_row, row_ids)
+
+        finish_near(i, 3)
         for c in range(3):
-            vel[c] = vel[c] - shared[c]
+            vel[c] = vel[c] - acc[c]
+
+        @pl.when(i < SUBSTEPS - 1)
+        def _():
+            advect(i + 1)
+
         return carry
 
     lax.fori_loop(0, SUBSTEPS, substep, 0)
 
     for c in range(3):
-        adv_out[c] = vel[c].reshape(8, 16, 128)
+        adv_out[c] = vel[c]
     divergence = left_dot(M_DZ, split(vel[0])) + left_dot(M_DX, split(vel[1]))
     divergence = divergence + right_dot(split(vel[2]), M_DY)
     source = (-SOURCE_GAIN / 4.0) * fields[0] * divergence
@@ -366,17 +428,20 @@
         parts = split(field)
         return sloc[...] - fields[0] * (left_dot(M_LEFT, parts) + right_dot(parts, M_RIGHT))
 
+    a_rows = 8 * len(a_ids)
+    b_rows = 16 * len(b_ids)
+
     def a_copies(it):
         return [
             pltpu.make_async_remote_copy(
                 src_ref=g1.at[it, slot],
                 dst_ref=g1.at[it, slot],
-                send_sem=a_send.at[it, k],
-                recv_sem=a_recv.at[it, k],
+                send_sem=a_send.at[it],
+                recv_sem=a_recv.at[it],
                 device_id=one,
                 device_id_type=MESH,
             )
-            for k, one in enumerate(a_ids)
+            for one in a_ids
         ]
 
     def b_copies(it):
@@ -384,12 +449,12 @@
             pltpu.make_async_remote_copy(
                 src_ref=g2.at[it, block],
                 dst_ref=g2.at[it, block],
-                send_sem=b_send.at[it, k],
-                recv_sem=b_recv.at[it, k],
+                send_sem=b_send.at[it],
+                recv_sem=b_recv.at[it],
                 device_id=one,
                 device_id_type=MESH,
             )
-            for k, one in enumerate(b_ids)
+            for one in b_ids
         ]
 
     def coarse_apply(pair):
@@ -410,21 +475,22 @@
         return jnp.sum(a[0] * b[0] + a[1] * b[1], keepdims=True)
 
     def conjugate(right_side):
-        solution = None
         residual = right_side
-        direction = right_side
+        image = coarse_apply(residual)
         norm_now = inner(residual, residual)
-        for sweep in range(COARSE_ITERS):
-            image = coarse_apply(direction)
-            alpha = norm_now / inner(direction, image)
-            step = [alpha * d for d in direction]
-            solution = step if solution is None else [x + d for x, d in zip(solution, step)]
-            if sweep == COARSE_ITERS - 1:
-                break
-            residual = [x - alpha * d for x, d in zip(residual, image)]
+        alpha = norm_now / inner(residual, image)
+        direction, moved = residual, image
+        solution = [alpha * d for d in direction]
+        for sweep in range(1, COARSE_ITERS):
+            residual = [x - alpha * d for x, d in zip(residual, moved)]
+            image = coarse_apply(residual)
             norm_next = inner(residual, residual)
+            energy = inner(residual, image)
             beta = norm_next / norm_now
+            alpha = norm_next / (energy - beta * norm_next / alpha)
             direction = [x + beta * d for x, d in zip(residual, direction)]
+            moved = [x + beta * d for x, d in zip(image, moved)]
+            solution = [x + alpha * d for x, d in zip(solution, direction)]
             norm_now = norm_next
         return solution
 
@@ -453,8 +519,7 @@
             copy.start()
         start_near(first, 1)
 
-        for copy in a_copies(it):
-            copy.wait_recv()
+        take(a_recv.at[it], a_rows)
         tops = []
         for j in range(4):
             tops.append(g1[it, 4 * j] + g1[it, 4 * j + 1] + (g1[it, 4 * j + 2] + g1[it, 4 * j + 3]))
@@ -471,14 +536,13 @@
         for copy in b_copies(it):
             copy.start()
 
-        shared = finish_near(first, 1)[0]
-        pressure = pressure + fields[2] * shared
+        finish_near(first, 1)
+        pressure = pressure + fields[2] * acc[0]
         pres[...] = pressure
         work[second, 0] = minus_laplace(pressure)
         start_near(second, 1)
 
-        for copy in b_copies(it):
-            copy.wait_recv()
+        take(b_recv.at[it], b_rows)
         right_side = []
         for half in range(2):
             at = slice(half * 8, half * 8 + 8)
@@ -521,29 +585,18 @@
         correction = right_dot(interp, M_JYT)
         applied = rows[2:3, :] * right_dot(image, M_JYT)
         applied = applied + fields[3] * right_dot(interp, M_KYT)
-        shared = finish_near(second, 1)[0]
-        pres[...] = pres[...] + correction + fields[2] * (shared - applied)
+        finish_near(second, 1)
+        pres[...] = pres[...] + correction + fields[2] * (acc[0] - applied)
         return carry
 
     lax.fori_loop(0, MG_ITERS, cycle, 0)
-    p_out[...] = pres[...].reshape(8, 16, 128)
-
-    def drain_substep(i, carry):
-        for copy in near_copies(i, 3):
-            copy.wait_send()
-        return carry
-
-    lax.fori_loop(0, SUBSTEPS, drain_substep, 0)
-
-    def drain_cycle(it, carry):
-        for r in (SUBSTEPS + 2 * it, SUBSTEPS + 2 * it + 1):
-            for copy in near_copies(r, 1):
-                copy.wait_send()
-        for copy in a_copies(it) + b_copies(it):
-            copy.wait_send()
-        return carry
-
-    lax.fori_loop(0, MG_ITERS, drain_cycle, 0)
+    p_out[...] = pres[...]
+
+    for r in range(ROUNDS):
+        take(n_send.at[r], near_rows(3 if r < SUBSTEPS else 1))
+    for it in range(MG_ITERS):
+        take(a_send.at[it], a_rows)
+        take(b_send.at[it], b_rows)
 
 
 def solution(mesh):
@@ -554,16 +607,21 @@
 
     def shards(velocity):
         vmem = pl.BlockSpec(memory_space=pltpu.VMEM)
-        return pl.pallas_call(
+        hbm = pl.BlockSpec(memory_space=pltpu.HBM)
+        advected, pressure = pl.pallas_call(
             functools.partial(kernel, (jz, kz, waz), count),
             out_shape=(
-                jax.ShapeDtypeStruct((3, 8, 16, 128), f32),
-                jax.ShapeDtypeStruct((8, 16, 128), f32),
+                jax.ShapeDtypeStruct((3, 128, 128), f32),
+                jax.ShapeDtypeStruct((128, 128), f32),
             ),
-            in_specs=[vmem] * 5,
+            in_specs=[hbm] * 5,
             out_specs=(vmem, vmem),
             scratch_shapes=[
                 pltpu.VMEM((3, 128, 128), f32),
+                pltpu.VMEM(matrices.shape, jnp.bfloat16),
+                pltpu.VMEM(fields.shape, f32),
+                pltpu.VMEM(rows.shape, f32),
+                pltpu.VMEM(spans.shape, f32),
                 pltpu.VMEM((128, 128), f32),
                 pltpu.VMEM((128, 128), f32),
                 pltpu.VMEM((8, 128), f32),
@@ -577,23 +635,28 @@
                 pltpu.VMEM((MG_ITERS, 16, 8, 128), f32),
                 pltpu.VMEM((MG_ITERS, blocks, 16, 128), f32),
                 pltpu.VMEM((2, count + 16, 128), f32),
-                pltpu.SemaphoreType.DMA((ROUNDS, 8)),
-                pltpu.SemaphoreType.DMA((ROUNDS, 8)),
-                pltpu.SemaphoreType.DMA((MG_ITERS, 15)),
-                pltpu.SemaphoreType.DMA((MG_ITERS, 15)),
-                pltpu.SemaphoreType.DMA((MG_ITERS, blocks - 1)),
-                pltpu.SemaphoreType.DMA((MG_ITERS, blocks - 1)),
+                pltpu.VMEM((240, 128), f32),
+                pltpu.SemaphoreType.DMA((5,)),
+                pltpu.SemaphoreType.DMA((ROUNDS,)),
+                pltpu.SemaphoreType.DMA((ROUNDS,)),
+                pltpu.SemaphoreType.DMA((MG_ITERS,)),
+                pltpu.SemaphoreType.DMA((MG_ITERS,)),
+                pltpu.SemaphoreType.DMA((MG_ITERS,)),
+                pltpu.SemaphoreType.DMA((MG_ITERS,)),
+                pltpu.SemaphoreType.REGULAR,
+                pltpu.SemaphoreType.REGULAR,
             ],
             compiler_params=pltpu.CompilerParams(
                 collective_id=0, has_side_effects=True, vmem_limit_bytes=32 * 1024 * 1024
             ),
         )(
-            velocity,
+            velocity.reshape(3, 128, 128),
             jnp.asarray(matrices),
             jnp.asarray(fields),
             jnp.asarray(rows),
             jnp.asarray(spans),
         )
+        return advected.reshape(3, 8, 16, 128), pressure.reshape(8, 16, 128)
 
     return jax.shard_map(
         shards,

time: 76.2 us -> 71 us (0.932)
  Pallas kernels: 69.4 us -> 64.2 us
    pallas_call x1, Pallas kernels: 69.4 us -> 64.2 us  [shards(): pl.pallas_call(functools.partial(kernel, (jz, kz, waz), count), out_shape...]
where the time goes in v2:
time: 71 us; the launch traced here: 70.7 us
  Pallas kernels  64.2 us (90%)
  local copies, waits for them, and re-layouts  5.88 us (8%)
    pallas_call x1, Pallas kernels, shards(): pl.pallas_call(functools.partial(kernel, (jz, kz, waz), count), out_shape...  64.2 us
    unnamed x12, local copies, waits for them, and re-layouts  5.88 us

profile of v2, /device:TPU:1, one launch (start us, length us, event | category | flops | bytes accessed | tf_op | source)
XLA Modules:
  0.0 70.7 jit_solution(9321589930037684912)
XLA Ops:
  0.6 0.0 copy-start.4
  0.6 0.7 copy-done.4
  1.3 0.0 copy-start
  1.3 1.1 %copy-done = bf16[10,2,128,128]{3,2,1,0:T(8,128)(2,1)S(1)} copy-done((bf16[10,2,128,128]{3,2,1,0:T(8,128)(2,1)S(1)}, bf16[10,2,128,128]{3,2,1,0:T(8,128)(2,1)}, u32[]{:S(2)}) %copy-start) | copy-done | bytes 655384
  2.4 0.0 copy-start.1
  2.4 0.9 %copy-done.1 = f32[4,128,128]{2,1,0:T(8,128)S(1)} copy-done((f32[4,128,128]{2,1,0:T(8,128)S(1)}, f32[4,128,128]{2,1,0:T(8,128)}, u32[]{:S(2)}) %copy-start.1) | copy-done | bytes 262168
  3.4 0.0 copy-start.2
  3.4 0.9 %copy-done.2 = f32[3,8,16,128]{3,2,1,0:T(8,128)S(1)} copy-done((f32[3,8,16,128]{3,2,1,0:T(8,128)S(1)}, f32[3,8,16,128]{3,2,1,0:T(8,128)}, u32[]{:S(2)}) %copy-start.2) | copy-done | bytes 196632
  4.3 0.0 copy-start.3
  4.3 0.9 %copy-done.3 = f32[4,6,16,128]{3,2,1,0:T(8,128)S(1)} copy-done((f32[4,6,16,128]{3,2,1,0:T(8,128)S(1)}, f32[4,6,16,128]{3,2,1,0:T(8,128)}, u32[]{:S(2)}) %copy-start.3) | copy-done | bytes 196632
  5.2 64.2 %shard_map.68 = (f32[3,128,128]{2,1,0:T(8,128)S(1)}, f32[128,128]{1,0:T(8,128)S(1)}) custom-call(f32[3,128,128]{2,1,0:T(8,128)S(1)} %bitcast.3, bf16[10,2,128,128]{3,2,1,0:T(8,128)(2,1)S(1)} %copy-done, f32[4,128,128]{2,1,0:T(8,128)S(1)} %copy-done.1, f32[8,128]{1,0:T(8,128)S(1)} %copy-done.4, f32[4,6,16,128]{3,2,1,0:T(8,128)S(1)} %copy-done.3), custom_call_target="tpu_custom_call" | custom-call | tf_op jit(solution)/shard_map/pallas_call | solution.py:611
  69.4 0.7 copy.9
  70.1 0.6 copy.10
Async XLA Ops:
  0.6 0.7 copy-start.4
  1.3 1.1 %copy-start = (bf16[10,2,128,128]{3,2,1,0:T(8,128)(2,1)S(1)}, bf16[10,2,128,128]{3,2,1,0:T(8,128)(2,1)}, u32[]{:S(2)}) copy-start(bf16[10,2,128,128]{3,2,1,0:T(8,128)(2,1)} %constant.8.clone.mats_in) | copy-start | bytes 1966084
  2.4 0.9 %copy-start.1 = (f32[4,128,128]{2,1,0:T(8,128)S(1)}, f32[4,128,128]{2,1,0:T(8,128)}, u32[]{:S(2)}) copy-start(f32[4,128,128]{2,1,0:T(8,128)} %constant.9.clone.fields_in) | copy-start | bytes 786436
  3.4 0.9 %copy-start.2 = (f32[3,8,16,128]{3,2,1,0:T(8,128)S(1)}, f32[3,8,16,128]{3,2,1,0:T(8,128)}, u32[]{:S(2)}) copy-start(f32[3,8,16,128]{3,2,1,0:T(8,128)} %param.5) | copy-start | bytes 589828
  4.3 0.9 %copy-start.3 = (f32[4,6,16,128]{3,2,1,0:T(8,128)S(1)}, f32[4,6,16,128]{3,2,1,0:T(8,128)}, u32[]{:S(2)}) copy-start(f32[4,6,16,128]{3,2,1,0:T(8,128)} %constant.11.clone.spans_in) | copy-start | bytes 589828

commit v3 on v2

--- a/solution.py
+++ b/solution.py
@@ -21,6 +21,7 @@
 
 MESH = pl.DeviceIdType.MESH
 ROUNDS = SUBSTEPS + 2 * MG_ITERS
+WALL_LANES = [95, 111, 127, 94, 110]
 
 
 def legendre_last(points, degree):
@@ -114,7 +115,14 @@
 
     def lanes(table):
         out = np.zeros((table.shape[0], 128))
-        out[:, :68] = np.tile(table, (1, 4))
+        out[:, :80] = np.tile(table[:, :16], (1, 5))
+        out[:, WALL_LANES] = table[:, 16:17]
+        return out
+
+    def across(table):
+        out = np.zeros((table.shape[0], 128))
+        out[:, :80] = np.repeat(table, 16, axis=1)
+        out[:, WALL_LANES] = table
         return out
 
     left = kron(scaled, eye(16)) + kron(eye(8), kron(eye(2), scaled)) + SHIFT_COEF / 4.0 * eye(128)
@@ -140,27 +148,20 @@
         ]
     ).astype(np.float32)
     lane = np.arange(128)
-    inner = lane % POINTS
-    level = lane % 17
-    valid = lane < 68
-    rows = np.zeros((8, 128), np.float32)
-    rows[0] = (inner == 0) & (lane > 0)
-    rows[1] = (inner == POINTS - 1) & (lane < 127)
-    rows[2] = way
-    rows[3] = np.where(valid, np.where((level == 0) | (level == 16), 1.0, 2.0), 0.0)
-    rows[4] = valid & (level < 16)
-    rows[5] = valid & (level > 0)
+    level = lane % 16
+    rows = np.zeros((32, 128), np.float32)
+    rows[0] = way
+    rows[1] = np.where(level == 0, 1.0, 2.0)
+    rows[2] = level < 15
+    rows[3] = level > 0
+    rows[4] = level == 15
+    for k in range(5):
+        spot = lane if k == 4 else (lane - 32 * k + 16) % 128
+        rows[8 + 3 * k] = spot < 80
+        rows[9 + 3 * k] = (spot >= 80) & (spot % 16 == 15)
+        rows[10 + 3 * k] = (spot >= 80) & (spot < 112) & (spot % 16 == 14)
     kinds = [jx, wax[:, None] * jx, 0.5 * kx + SHIFT_COEF / 8.0 * wax[:, None] * jx]
-    spans = np.zeros((4, 6, 16, 128), np.float32)
-    for sub in range(4):
-        for kind, table in enumerate(kinds):
-            for half in range(2):
-                for slot in range(4):
-                    column = (2 * slot + half - 2 * sub + 1) % 8
-                    if column < 5:
-                        spans[sub, kind * 2 + half, :, slot * 17 : slot * 17 + 17] = table[
-                            :, column : column + 1
-                        ]
+    spans = np.stack([across(one) for one in kinds]).astype(np.float32)
     return matrices, fields, rows, spans, jz, kz, waz
 
 
@@ -207,21 +208,22 @@
     known_row,
 ):
     jz, kz, waz = zcoef
-    blocks = count // 4
-    tiles = blocks // 2
+    planes = count // 16
     elem = lax.axis_index("elem")
     sub = lax.axis_index("sub")
-    block = elem // 4
-    place = elem % 4
-    slot = place * 4 + sub
+    plane = elem // 16
+    place = elem % 16
+    slot = plane * 4 + sub
+    turn = lax.rem(32 * sub + 112, 128)
 
     def near(de, ds):
         return (lax.rem(elem + de + count, count), lax.rem(sub + ds + 4, 4))
 
-    def at_block(dx, dz):
-        bx, bz = block // 4, block % 4
-        other = lax.rem(bx + dx, blocks // 4) * 4 + lax.rem(bz + dz, 4)
-        return (other * 4 + place, sub)
+    def along(dj):
+        return (plane * 16 + lax.rem(place + dj, 16), sub)
+
+    def over(dx, ds):
+        return (lax.rem(plane + dx, planes) * 16 + place, lax.rem(sub + ds, 4))
 
     near_ids = [
         near(1, 1),
@@ -233,20 +235,12 @@
         near(0, 1),
         near(0, -1),
     ]
-    a_ids = [
-        (block * 4 + lax.rem(place + dj, 4), lax.rem(sub + ds, 4))
-        for ds in (2, 1, 3, 0)
-        for dj in (2, 1, 3, 0)
-        if dj or ds
-    ]
-    b_ids = [
-        at_block(dx, dz)
-        for dz in (2, 1, 3, 0)
-        for dx in (2, 1, 3, 0)
-        if (dx or dz) and dx < blocks // 4
-    ]
-    row_ids = [at_block(dx, 0) for dx in range(1, blocks // 4)]
-    side_ids = [at_block(0, 1), at_block(0, 3)]
+    a_ids = [along(dj) for dj in sorted(range(1, 16), key=lambda d: -min(d, 16 - d))]
+    steps = [(dx, ds) for dx in range(planes) for ds in range(4) if dx or ds]
+    steps = sorted(steps, key=lambda d: -(min(d[0], planes - d[0]) + min(d[1], 4 - d[1])))
+    b_ids = [over(dx, ds) for dx, ds in steps]
+    side_ids = [along(4), along(12)]
+    row_ids = [over(dx, 0) for dx in range(1, planes)]
 
     loads = [
         pltpu.make_async_copy(src, dst, load.at[k])
@@ -257,7 +251,7 @@
     for copy in loads:
         copy.start()
     barrier = pltpu.get_barrier_semaphore()
-    partners = near_ids + side_ids + row_ids
+    partners = near_ids + side_ids + [along(2), along(14)] + row_ids
     for one in partners:
         pl.semaphore_signal(barrier, inc=1, device_id=one, device_id_type=MESH)
 
@@ -394,26 +388,6 @@
 
     for c in range(3):
         adv_out[c] = vel[c]
-    divergence = left_dot(M_DZ, split(vel[0])) + left_dot(M_DX, split(vel[1]))
-    divergence = divergence + right_dot(split(vel[2]), M_DY)
-    source = (-SOURCE_GAIN / 4.0) * fields[0] * divergence
-    sloc[...] = source
-    pres[...] = jnp.zeros_like(source)
-    direct = right_dot(split(source), M_JY).reshape(8, 16, 128)
-    for half in range(2):
-        span = spans[sub, half]
-        for zi in range(4):
-            total = None
-            for z in range(8):
-                if jz[z, zi] != 0.0:
-                    one = float(jz[z, zi]) * direct[z]
-                    total = one if total is None else total + one
-            if total is None:
-                row = jnp.zeros((1, 128), jnp.float32)
-            else:
-                row = jnp.sum(total * span, axis=0, keepdims=True)
-            csrc[half * 4 + zi : half * 4 + zi + 1, :] = row
-
     def weighted(table, zi, field):
         total = None
         for z in range(8):
@@ -422,6 +396,16 @@
                 total = one if total is None else total + one
         return total
 
+    divergence = left_dot(M_DZ, split(vel[0])) + left_dot(M_DX, split(vel[1]))
+    divergence = divergence + right_dot(split(vel[2]), M_DY)
+    source = (-SOURCE_GAIN / 4.0) * fields[0] * divergence
+    sloc[...] = source
+    pres[...] = jnp.zeros_like(source)
+    direct = right_dot(split(source), M_JY).reshape(8, 16, 128)
+    for zi in (1, 2):
+        row = jnp.sum(weighted(jz, zi, direct) * spans[0], axis=0, keepdims=True)
+        csrc[zi : zi + 1, :] = row
+
     wjz = waz[:, None] * jz
 
     def minus_laplace(field):
@@ -429,13 +413,13 @@
         return sloc[...] - fields[0] * (left_dot(M_LEFT, parts) + right_dot(parts, M_RIGHT))
 
     a_rows = 8 * len(a_ids)
-    b_rows = 16 * len(b_ids)
+    b_rows = 24 * len(b_ids)
 
     def a_copies(it):
         return [
             pltpu.make_async_remote_copy(
-                src_ref=g1.at[it, slot],
-                dst_ref=g1.at[it, slot],
+                src_ref=g1.at[it, place],
+                dst_ref=g1.at[it, place],
                 send_sem=a_send.at[it],
                 recv_sem=a_recv.at[it],
                 device_id=one,
@@ -447,8 +431,8 @@
     def b_copies(it):
         return [
             pltpu.make_async_remote_copy(
-                src_ref=g2.at[it, block],
-                dst_ref=g2.at[it, block],
+                src_ref=g2.at[it, slot],
+                dst_ref=g2.at[it, slot],
                 send_sem=b_send.at[it],
                 recv_sem=b_recv.at[it],
                 device_id=one,
@@ -458,18 +442,16 @@
         ]
 
     def coarse_apply(pair):
-        my, up, down = rows[3:4, :], rows[4:5, :], rows[5:6, :]
-        even, odd = pair
-        across = (
-            odd + pltpu.roll(odd, 17, 1) + pltpu.roll(odd, 77, 1),
-            even + pltpu.roll(even, 111, 1) + pltpu.roll(even, 51, 1),
-        )
-        out = []
-        for u, near_x in zip(pair, across):
-            near_z = pltpu.roll(u, 1, 0) + pltpu.roll(u, u.shape[0] - 1, 0)
-            one = my * (3.025 * u - 0.5 * (near_z + near_x))
-            out.append(one - up * pltpu.roll(u, 127, 1) - down * pltpu.roll(u, 1, 1))
-        return out
+        my, up, down, top = rows[1:2, :], rows[2:3, :], rows[3:4, :], rows[4:5, :]
+
+        def middle(u):
+            near_x = pltpu.roll(u, 16, 1) + pltpu.roll(u, 112, 1)
+            near_z = pltpu.roll(u, 1, 0) + pltpu.roll(u, count - 1, 0)
+            return 3.025 * u - 0.5 * (near_z + near_x)
+
+        u, wall = pair
+        body = my * middle(u) - up * pltpu.roll(u, 127, 1) - down * pltpu.roll(u, 1, 1)
+        return [body - top * wall, top * (middle(wall) - u)]
 
     def inner(a, b):
         return jnp.sum(a[0] * b[0] + a[1] * b[1], keepdims=True)
@@ -503,36 +485,39 @@
         mixed = split(pressure * fields[1] + fields[2] * local)
         flat = right_dot(mixed, M_JYW).reshape(8, 16, 128)
         bent = right_dot(mixed, M_KY).reshape(8, 16, 128)
+        tile = jnp.zeros((8, 128), jnp.float32)
         for zi in range(4):
-            edge = 0.5 * weighted(kz, zi, flat)
-            body = weighted(wjz, zi, flat)
-            if body is not None:
-                edge = edge + 0.5 * weighted(wjz, zi, bent)
-            for half in range(2):
-                total = edge * spans[sub, 2 + half]
-                if body is not None:
-                    total = total + body * spans[sub, 4 + half]
-                at = half * 4 + zi
-                row = jnp.sum(total, axis=0, keepdims=True)
-                g1[it, slot, at : at + 1, :] = csrc[at : at + 1, :] - row
+            total = (0.5 * weighted(kz, zi, flat)) * spans[1]
+            if zi in (1, 2):
+                total = total + (0.5 * weighted(wjz, zi, bent)) * spans[1]
+                total = total + weighted(wjz, zi, flat) * spans[2]
+            row = -jnp.sum(total, axis=0, keepdims=True)
+            if zi in (1, 2):
+                row = csrc[zi : zi + 1, :] + row
+            tile = jnp.where(sublane == lax.rem(place + zi + 7, 8), row, tile)
+        g1[it, place] = tile
         for copy in a_copies(it):
             copy.start()
         start_near(first, 1)
 
         take(a_recv.at[it], a_rows)
-        tops = []
-        for j in range(4):
-            tops.append(g1[it, 4 * j] + g1[it, 4 * j + 1] + (g1[it, 4 * j + 2] + g1[it, 4 * j + 3]))
-        odd_block = lax.rem(block, 2) == 1
-        for half in range(2):
-            total = None
-            for j in range(4):
-                shift = (j - 4 * half) % 8
-                moved = pltpu.roll(tops[j], shift, 0) if shift else tops[j]
-                moved = jnp.where((sublane >= j) & (sublane < j + 4), moved, 0.0)
-                total = moved if total is None else total + moved
-            total = jnp.where(odd_block, pltpu.roll(total, 3, 0), pltpu.roll(total, 7, 0))
-            g2[it, block, half * 8 : half * 8 + 8, :] = total
+        lower, upper = sublane < 4, sublane >= 4
+
+        def some(mask, x):
+            return jnp.where(mask, x, 0.0)
+
+        first_edge = g1[it, 6] + g1[it, 7] + g1[it, 8]
+        last_edge = g1[it, 14] + g1[it, 15]
+        base = g1[it, 0]
+        tops = [
+            (g1[it, 1] + g1[it, 2]) + (g1[it, 3] + g1[it, 4]) + (g1[it, 5] + some(lower, base))
+            + some(upper, first_edge),
+            (g1[it, 9] + g1[it, 10]) + (g1[it, 11] + g1[it, 12]) + g1[it, 13]
+            + (some(lower, first_edge) + some(upper, last_edge)),
+            some(lower, last_edge) + some(upper, base),
+        ]
+        for k in range(3):
+            g2[it, slot, 8 * k : 8 * k + 8, :] = pltpu.roll(tops[k], turn, 1)
         for copy in b_copies(it):
             copy.start()
 
@@ -543,47 +528,53 @@
         start_near(second, 1)
 
         take(b_recv.at[it], b_rows)
-        right_side = []
-        for half in range(2):
-            at = slice(half * 8, half * 8 + 8)
-            pieces = []
-            for t in range(tiles):
-                one = jnp.where(sublane < 6, g2[it, 2 * t, at, :], 0.0)
-                one = one + jnp.where(sublane >= 3, g2[it, 2 * t + 1, at, :], 0.0)
-                one = one + jnp.where(sublane == 7, g2[it, (2 * t + 2) % blocks, at, :], 0.0)
-                one = one + jnp.where(sublane < 2, g2[it, (2 * t - 1) % blocks, at, :], 0.0)
-                pieces.append(one)
-            right_side.append(jnp.concatenate(pieces, axis=0))
+        pieces, walls = [], []
+        for x in range(planes):
+            before, after = (x - 1) % planes, (x + 1) % planes
+            for k in range(2):
+                sums = [None] * 3
+                for sy in range(4):
+                    one = g2[it, 4 * x + sy, 8 * k : 8 * k + 8, :]
+                    if k == 0:
+                        one = one + some(lower, g2[it, 4 * before + sy, 16:24, :])
+                    else:
+                        one = one + some(upper, g2[it, 4 * after + sy, 16:24, :])
+                    for n in range(3):
+                        at = 8 + 3 * sy + n
+                        part = one * rows[at : at + 1, :]
+                        sums[n] = part if sums[n] is None else sums[n] + part
+                pieces.append(sums[0])
+                walls.append(pltpu.roll(sums[1], 48, 1) + pltpu.roll(sums[2], 97, 1))
+        right_side = [jnp.concatenate(pieces, axis=0), jnp.concatenate(walls, axis=0)]
         answer = conjugate(right_side)
-        vertex = []
         for half in range(2):
             ext[half, 0:8] = answer[half][count - 8 : count]
             ext[half, 8 : 8 + count] = answer[half]
             ext[half, 8 + count : 16 + count] = answer[half][0:8]
-            vertex.append([ext[half, pl.ds(elem + 7 + v, 1), :] for v in range(4)])
+        body = ext[0, pl.ds(elem + 7, 8), :]
+        wall = ext[1, pl.ds(elem + 7, 8), :]
+        own = rows[20:21, :] * pltpu.roll(body, lax.rem(256 - turn, 128), 1)
+        own = own + rows[21:22, :] * pltpu.roll(wall, lax.rem(208 - turn, 128), 1)
+        own = own + rows[22:23, :] * pltpu.roll(wall, lax.rem(159 - turn, 128), 1)
+        vertex = [own[v : v + 1, :] for v in range(4)]
 
         interp, image = [], []
         for z in range(8):
-            one, two = None, None
-            for half in range(2):
-                value = float(jz[z, 1]) * vertex[half][1] + float(jz[z, 2]) * vertex[half][2]
-                part = value * spans[sub, half]
-                one = part if one is None else one + part
-                part = (float(waz[z]) * value) * spans[sub, 4 + half]
-                if np.any(kz[z] != 0.0):
-                    bend = None
-                    for v in range(4):
-                        if kz[z, v] != 0.0:
-                            term = (0.5 * float(kz[z, v])) * vertex[half][v]
-                            bend = term if bend is None else bend + term
-                    part = part + bend * spans[sub, 2 + half]
-                two = part if two is None else two + part
-            interp.append(one)
-            image.append(two)
+            value = float(jz[z, 1]) * vertex[1] + float(jz[z, 2]) * vertex[2]
+            interp.append(value * spans[0])
+            part = (float(waz[z]) * value) * spans[2]
+            if np.any(kz[z] != 0.0):
+                bend = None
+                for v in range(4):
+                    if kz[z, v] != 0.0:
+                        term = (0.5 * float(kz[z, v])) * vertex[v]
+                        bend = term if bend is None else bend + term
+                part = part + bend * spans[1]
+            image.append(part)
         interp = split(jnp.concatenate(interp, axis=0))
         image = split(jnp.concatenate(image, axis=0))
         correction = right_dot(interp, M_JYT)
-        applied = rows[2:3, :] * right_dot(image, M_JYT)
+        applied = rows[0:1, :] * right_dot(image, M_JYT)
         applied = applied + fields[3] * right_dot(interp, M_KYT)
         finish_near(second, 1)
         pres[...] = pres[...] + correction + fields[2] * (acc[0] - applied)
@@ -602,7 +593,7 @@
 def solution(mesh):
     count = mesh.shape["elem"]
     matrices, fields, rows, spans, jz, kz, waz = make_tables()
-    blocks = count // 4
+    planes = count // 16
     f32 = jnp.float32
 
     def shards(velocity):
@@ -633,9 +624,9 @@
                 pltpu.VMEM((ROUNDS, 2, 3, 8, 128), f32),
                 pltpu.VMEM((ROUNDS, 4, 8, 128), f32),
                 pltpu.VMEM((MG_ITERS, 16, 8, 128), f32),
-                pltpu.VMEM((MG_ITERS, blocks, 16, 128), f32),
+                pltpu.VMEM((MG_ITERS, 4 * planes, 24, 128), f32),
                 pltpu.VMEM((2, count + 16, 128), f32),
-                pltpu.VMEM((240, 128), f32),
+                pltpu.VMEM((360, 128), f32),
                 pltpu.SemaphoreType.DMA((5,)),
                 pltpu.SemaphoreType.DMA((ROUNDS,)),
                 pltpu.SemaphoreType.DMA((ROUNDS,)),
@@ -647,7 +638,7 @@
                 pltpu.SemaphoreType.REGULAR,
             ],
             compiler_params=pltpu.CompilerParams(
-                collective_id=0, has_side_effects=True, vmem_limit_bytes=32 * 1024 * 1024
+                collective_id=0, has_side_effects=True, vmem_limit_bytes=60 * 1024 * 1024
             ),
         )(
             velocity.reshape(3, 128, 128),

time: 71 us -> 64.8 us (0.913)
  local copies, waits for them, and re-layouts: 5.88 us -> 2.28 us
  Pallas kernels: 64.2 us -> 61.8 us
    unnamed x12 -> x4, local copies, waits for them, and re-layouts: 5.88 us -> 2.28 us
    pallas_call x1, Pallas kernels: 64.2 us -> 61.8 us  [shards(): pl.pallas_call(functools.partial(kernel, (jz, kz, waz), count), out_shape...]
where the time goes in v3:
time: 64.8 us; the launch traced here: 64.7 us
  Pallas kernels  61.8 us (95%)
  local copies, waits for them, and re-layouts  2.28 us (4%)
  between operations  0.65 us (1%)
    pallas_call x1, Pallas kernels, shards(): pl.pallas_call(functools.partial(kernel, (jz, kz, waz), count), out_shape...  61.8 us
    unnamed x4, local copies, waits for them, and re-layouts  2.28 us

profile of v3, /device:TPU:1, one launch (start us, length us, event | category | flops | bytes accessed | tf_op | source)
XLA Modules:
  0.0 64.7 jit_solution(5992194123048963132)
XLA Ops:
  0.6 61.8 %shard_map.68 = (f32[3,128,128]{2,1,0:T(8,128)}, f32[128,128]{1,0:T(8,128)}) custom-call(f32[3,128,128]{2,1,0:T(8,128)} %bitcast.3, bf16[10,2,128,128]{3,2,1,0:T(8,128)(2,1)} %constant.8.clone.mats_in, f32[4,128,128]{2,1,0:T(8,128)} %constant.9.clone.fields_in, f32[32,128]{1,0:T(8,128)} %constant.10.clone.rows_in, f32[3,16,128]{2,1,0:T(8,128)} %constant.11.clone.spans_in), custom_call_target="tpu_custom_call" | custom-call | tf_op jit(solution)/shard_map/pallas_call | solution.py:602
  62.4 0.0 copy-start
  62.4 1.6 %copy.9 = f32[3,8,16,128]{3,2,1,0:T(8,128)} copy(f32[3,8,16,128]{3,2,1,0:T(8,128)} %bitcast.4) | data formatting | bytes 393216
  64.1 0.0 copy-done
  64.1 0.6 copy.10
Async XLA Ops:
  62.4 1.7 %copy-start = (f32[128,128]{1,0:T(8,128)S(1)}, f32[128,128]{1,0:T(8,128)}, u32[]{:S(2)}) copy-start(f32[128,128]{1,0:T(8,128)} %get-tuple-element.5) | copy-start | bytes 196612

commit v4 on v3

--- a/solution.py
+++ b/solution.py
@@ -162,7 +162,8 @@
         rows[10 + 3 * k] = (spot >= 80) & (spot < 112) & (spot % 16 == 14)
     kinds = [jx, wax[:, None] * jx, 0.5 * kx + SHIFT_COEF / 8.0 * wax[:, None] * jx]
     spans = np.stack([across(one) for one in kinds]).astype(np.float32)
-    return matrices, fields, rows, spans, jz, kz, waz
+    small = np.concatenate([fields.reshape(-1, 128), rows, spans.reshape(-1, 128)])
+    return matrices, small, jz, kz, waz
 
 
 M_DZ, M_DX, M_DY, M_LEFT, M_RIGHT, M_JYW, M_KY, M_JY, M_JYT, M_KYT = range(10)
@@ -173,16 +174,12 @@
     count,
     vel_in,
     mats_in,
-    fields_in,
-    rows_in,
-    spans_in,
+    small_in,
     adv_out,
     p_out,
     vel,
     mats,
-    fields,
-    rows,
-    spans,
+    small,
     sloc,
     pres,
     csrc,
@@ -209,6 +206,9 @@
 ):
     jz, kz, waz = zcoef
     planes = count // 16
+    fields = [small.at[pl.ds(128 * k, 128)] for k in range(4)]
+    rows = small.at[pl.ds(512, 32)]
+    spans = [small.at[pl.ds(544 + 16 * k, 16)] for k in range(3)]
     elem = lax.axis_index("elem")
     sub = lax.axis_index("sub")
     plane = elem // 16
@@ -245,15 +245,15 @@
     loads = [
         pltpu.make_async_copy(src, dst, load.at[k])
         for k, (src, dst) in enumerate(
-            ((vel_in, vel), (mats_in, mats), (fields_in, fields), (rows_in, rows), (spans_in, spans))
+            ((vel_in, vel), (mats_in, mats), (small_in, small))
         )
     ]
-    for copy in loads:
-        copy.start()
     barrier = pltpu.get_barrier_semaphore()
     partners = near_ids + side_ids + [along(2), along(14)] + row_ids
     for one in partners:
         pl.semaphore_signal(barrier, inc=1, device_id=one, device_id_type=MESH)
+    for copy in loads:
+        copy.start()
 
     sublane = lax.broadcasted_iota(jnp.int32, (8, 128), 0)
     lane = lax.broadcasted_iota(jnp.int32, (1, 128), 1)
@@ -305,7 +305,7 @@
     def near_rows(comps):
         return 32 + 48 * comps
 
-    def start_near(r, comps):
+    def stage_near(r, comps):
         for corner, row in enumerate((127, 112, 15, 0)):
             tile = jnp.zeros((8, 128), jnp.float32)
             for c in range(comps):
@@ -314,7 +314,9 @@
         for c in range(comps):
             xs[r, 0, c] = work[r, c, pl.ds(0, 8, stride=16), :]
             xs[r, 1, c] = work[r, c, pl.ds(15, 8, stride=16), :]
-        for copy in near_copies(r, comps):
+
+    def send_near(r, comps, part=slice(None)):
+        for copy in near_copies(r, comps)[part]:
             copy.start()
 
     def share_y(field):
@@ -351,11 +353,12 @@
             term = vel[0] * left_dot(M_DZ, parts[c])
             term = term + vel[1] * left_dot(M_DX, parts[c])
             term = term + vel[2] * right_dot(parts[c], M_DY)
-            work[i, c] = term * ((2.0 * TIME_STEP) * fields[1])
+            work[i, c] = term * ((2.0 * TIME_STEP) * fields[1][...])
 
     for copy in loads:
         copy.wait()
     advect(0)
+    stage_near(0, 3)
     pl.semaphore_wait(barrier, len(partners))
 
     def pass_on(known, ids):
@@ -364,7 +367,7 @@
         pl.semaphore_wait(known, len(ids))
 
     def substep(i, carry):
-        start_near(i, 3)
+        send_near(i, 3)
 
         @pl.when(i == 0)
         def _():
@@ -381,6 +384,7 @@
         @pl.when(i < SUBSTEPS - 1)
         def _():
             advect(i + 1)
+            stage_near(i + 1, 3)
 
         return carry
 
@@ -398,19 +402,19 @@
 
     divergence = left_dot(M_DZ, split(vel[0])) + left_dot(M_DX, split(vel[1]))
     divergence = divergence + right_dot(split(vel[2]), M_DY)
-    source = (-SOURCE_GAIN / 4.0) * fields[0] * divergence
+    source = (-SOURCE_GAIN / 4.0) * fields[0][...] * divergence
     sloc[...] = source
     pres[...] = jnp.zeros_like(source)
     direct = right_dot(split(source), M_JY).reshape(8, 16, 128)
     for zi in (1, 2):
-        row = jnp.sum(weighted(jz, zi, direct) * spans[0], axis=0, keepdims=True)
+        row = jnp.sum(weighted(jz, zi, direct) * spans[0][...], axis=0, keepdims=True)
         csrc[zi : zi + 1, :] = row
 
     wjz = waz[:, None] * jz
 
     def minus_laplace(field):
         parts = split(field)
-        return sloc[...] - fields[0] * (left_dot(M_LEFT, parts) + right_dot(parts, M_RIGHT))
+        return sloc[...] - fields[0][...] * (left_dot(M_LEFT, parts) + right_dot(parts, M_RIGHT))
 
     a_rows = 8 * len(a_ids)
     b_rows = 24 * len(b_ids)
@@ -454,25 +458,37 @@
         return [body - top * wall, top * (middle(wall) - u)]
 
     def inner(a, b):
-        return jnp.sum(a[0] * b[0] + a[1] * b[1], keepdims=True)
+        total = jnp.sum((a[0] * b[0]).reshape(count // 8, 8, 128), axis=0)
+        total = total + jnp.sum((a[1] * b[1]).reshape(-1, 8, 128), axis=0)
+        return jnp.sum(jnp.sum(total, axis=0, keepdims=True), axis=1, keepdims=True)
+
+    def plus(a, factor, b):
+        return [x + factor * y for x, y in zip(a, b)]
 
     def conjugate(right_side):
         residual = right_side
         image = coarse_apply(residual)
         norm_now = inner(residual, residual)
-        alpha = norm_now / inner(residual, image)
-        direction, moved = residual, image
+        energy = inner(residual, image)
+        further = coarse_apply(image)
+        alpha = norm_now / energy
+        direction, moved, twice = residual, image, further
         solution = [alpha * d for d in direction]
         for sweep in range(1, COARSE_ITERS):
-            residual = [x - alpha * d for x, d in zip(residual, moved)]
-            image = coarse_apply(residual)
+            residual = plus(residual, -alpha, moved)
+            image = plus(image, -alpha, twice)
             norm_next = inner(residual, residual)
             energy = inner(residual, image)
+            more = sweep < COARSE_ITERS - 1
+            if more:
+                further = coarse_apply(image)
             beta = norm_next / norm_now
             alpha = norm_next / (energy - beta * norm_next / alpha)
-            direction = [x + beta * d for x, d in zip(residual, direction)]
-            moved = [x + beta * d for x, d in zip(image, moved)]
-            solution = [x + alpha * d for x, d in zip(solution, direction)]
+            direction = plus(residual, beta, direction)
+            solution = plus(solution, alpha, direction)
+            if more:
+                moved = plus(image, beta, moved)
+                twice = plus(further, beta, twice)
             norm_now = norm_next
         return solution
 
@@ -482,15 +498,15 @@
         pressure = pres[...]
         local = minus_laplace(pressure)
         work[first, 0] = local
-        mixed = split(pressure * fields[1] + fields[2] * local)
+        mixed = split(pressure * fields[1][...] + fields[2][...] * local)
         flat = right_dot(mixed, M_JYW).reshape(8, 16, 128)
         bent = right_dot(mixed, M_KY).reshape(8, 16, 128)
         tile = jnp.zeros((8, 128), jnp.float32)
         for zi in range(4):
-            total = (0.5 * weighted(kz, zi, flat)) * spans[1]
+            total = (0.5 * weighted(kz, zi, flat)) * spans[1][...]
             if zi in (1, 2):
-                total = total + (0.5 * weighted(wjz, zi, bent)) * spans[1]
-                total = total + weighted(wjz, zi, flat) * spans[2]
+                total = total + (0.5 * weighted(wjz, zi, bent)) * spans[1][...]
+                total = total + weighted(wjz, zi, flat) * spans[2][...]
             row = -jnp.sum(total, axis=0, keepdims=True)
             if zi in (1, 2):
                 row = csrc[zi : zi + 1, :] + row
@@ -498,7 +514,8 @@
         g1[it, place] = tile
         for copy in a_copies(it):
             copy.start()
-        start_near(first, 1)
+        stage_near(first, 1)
+        send_near(first, 1)
 
         take(a_recv.at[it], a_rows)
         lower, upper = sublane < 4, sublane >= 4
@@ -522,10 +539,11 @@
             copy.start()
 
         finish_near(first, 1)
-        pressure = pressure + fields[2] * acc[0]
+        pressure = pressure + fields[2][...] * acc[0]
         pres[...] = pressure
         work[second, 0] = minus_laplace(pressure)
-        start_near(second, 1)
+        stage_near(second, 1)
+        send_near(second, 1)
 
         take(b_recv.at[it], b_rows)
         pieces, walls = [], []
@@ -561,23 +579,23 @@
         interp, image = [], []
         for z in range(8):
             value = float(jz[z, 1]) * vertex[1] + float(jz[z, 2]) * vertex[2]
-            interp.append(value * spans[0])
-            part = (float(waz[z]) * value) * spans[2]
+            interp.append(value * spans[0][...])
+            part = (float(waz[z]) * value) * spans[2][...]
             if np.any(kz[z] != 0.0):
                 bend = None
                 for v in range(4):
                     if kz[z, v] != 0.0:
                         term = (0.5 * float(kz[z, v])) * vertex[v]
                         bend = term if bend is None else bend + term
-                part = part + bend * spans[1]
+                part = part + bend * spans[1][...]
             image.append(part)
         interp = split(jnp.concatenate(interp, axis=0))
         image = split(jnp.concatenate(image, axis=0))
         correction = right_dot(interp, M_JYT)
         applied = rows[0:1, :] * right_dot(image, M_JYT)
-        applied = applied + fields[3] * right_dot(interp, M_KYT)
+        applied = applied + fields[3][...] * right_dot(interp, M_KYT)
         finish_near(second, 1)
-        pres[...] = pres[...] + correction + fields[2] * (acc[0] - applied)
+        pres[...] = pres[...] + correction + fields[2][...] * (acc[0] - applied)
         return carry
 
     lax.fori_loop(0, MG_ITERS, cycle, 0)
@@ -592,7 +610,7 @@
 
 def solution(mesh):
     count = mesh.shape["elem"]
-    matrices, fields, rows, spans, jz, kz, waz = make_tables()
+    matrices, small, jz, kz, waz = make_tables()
     planes = count // 16
     f32 = jnp.float32
 
@@ -605,14 +623,12 @@
                 jax.ShapeDtypeStruct((3, 128, 128), f32),
                 jax.ShapeDtypeStruct((128, 128), f32),
             ),
-            in_specs=[hbm] * 5,
+            in_specs=[hbm] * 3,
             out_specs=(vmem, vmem),
             scratch_shapes=[
                 pltpu.VMEM((3, 128, 128), f32),
                 pltpu.VMEM(matrices.shape, jnp.bfloat16),
-                pltpu.VMEM(fields.shape, f32),
-                pltpu.VMEM(rows.shape, f32),
-                pltpu.VMEM(spans.shape, f32),
+                pltpu.VMEM(small.shape, f32),
                 pltpu.VMEM((128, 128), f32),
                 pltpu.VMEM((128, 128), f32),
                 pltpu.VMEM((8, 128), f32),
@@ -627,7 +643,7 @@
                 pltpu.VMEM((MG_ITERS, 4 * planes, 24, 128), f32),
                 pltpu.VMEM((2, count + 16, 128), f32),
                 pltpu.VMEM((360, 128), f32),
-                pltpu.SemaphoreType.DMA((5,)),
+                pltpu.SemaphoreType.DMA((3,)),
                 pltpu.SemaphoreType.DMA((ROUNDS,)),
                 pltpu.SemaphoreType.DMA((ROUNDS,)),
                 pltpu.SemaphoreType.DMA((MG_ITERS,)),
@@ -638,14 +654,12 @@
                 pltpu.SemaphoreType.REGULAR,
             ],
             compiler_params=pltpu.CompilerParams(
-                collective_id=0, has_side_effects=True, vmem_limit_bytes=60 * 1024 * 1024
+                collective_id=0, has_side_effects=True, vmem_limit_bytes=54912 * 1024
             ),
         )(
             velocity.reshape(3, 128, 128),
             jnp.asarray(matrices),
-            jnp.asarray(fields),
-            jnp.asarray(rows),
-            jnp.asarray(spans),
+            jnp.asarray(small),
         )
         return advected.reshape(3, 8, 16, 128), pressure.reshape(8, 16, 128)
 

time: 64.8 us -> 61.9 us (0.955)
  Pallas kernels: 61.8 us -> 59.9 us
  local copies, waits for them, and re-layouts: 2.28 us -> 1.31 us
    pallas_call x1, Pallas kernels: 61.8 us -> 59.9 us  [shards(): pl.pallas_call(functools.partial(kernel, (jz, kz, waz), count), out_shape...]
    unnamed x4 -> x2, local copies, waits for them, and re-layouts: 2.28 us -> 1.31 us
where the time goes in v4:
time: 61.9 us; the launch traced here: 61.8 us
  Pallas kernels  59.9 us (97%)
  local copies, waits for them, and re-layouts  1.31 us (2%)
  between operations  0.64 us (1%)
    pallas_call x1, Pallas kernels, shards(): pl.pallas_call(functools.partial(kernel, (jz, kz, waz), count), out_shape...  59.9 us
    unnamed x2, local copies, waits for them, and re-layouts  1.31 us

profile of v4, /device:TPU:1, one launch (start us, length us, event | category | flops | bytes accessed | tf_op | source)
XLA Modules:
  0.0 61.8 jit_solution(719869437414138867)
XLA Ops:
  0.6 59.9 %shard_map.50 = (f32[3,128,128]{2,1,0:T(8,128)S(1)}, f32[128,128]{1,0:T(8,128)S(1)}) custom-call(f32[3,128,128]{2,1,0:T(8,128)} %bitcast.5, bf16[10,2,128,128]{3,2,1,0:T(8,128)(2,1)} %constant.4.clone.mats_in, f32[592,128]{1,0:T(8,128)} %constant.5.clone.small_in), custom_call_target="tpu_custom_call" | custom-call | tf_op jit(solution)/shard_map/pallas_call | solution.py:620
  60.5 0.7 %copy.7 = f32[3,8,16,128]{3,2,1,0:T(8,128)} copy(f32[3,8,16,128]{3,2,1,0:T(8,128)S(1)} %bitcast.3) | data formatting | bytes 393216
  61.2 0.6 %copy.8 = f32[8,16,128]{2,1,0:T(8,128)} copy(f32[8,16,128]{2,1,0:T(8,128)S(1)} %bitcast.4) | data formatting | bytes 131072

commit v5 on v4

--- a/solution.py
+++ b/solution.py
@@ -22,6 +22,9 @@
 MESH = pl.DeviceIdType.MESH
 ROUNDS = SUBSTEPS + 2 * MG_ITERS
 WALL_LANES = [95, 111, 127, 94, 110]
+
+
+CORNERS = (127, 112, 15, 0)
 
 
 def legendre_last(points, degree):
@@ -129,8 +132,8 @@
     matrices = [
         kron(deriv, eye(16)),
         kron(eye(8), kron(eye(2), deriv)),
+        left,
         kron(eye(16), deriv).T,
-        left,
         kron(eye(16), scaled).T,
         lanes(way[:, None] * jy),
         lanes(ky),
@@ -138,7 +141,11 @@
         lanes(jy).T,
         lanes(ky).T,
     ]
-    matrices = np.stack([halves(one) for one in matrices])
+    pairs = [halves(one) for one in matrices]
+    flat = [pairs[0][0], pairs[1][0], pairs[0][1], pairs[1][1]]
+    for pair in pairs[2:]:
+        flat.extend([pair[0], pair[1]])
+    matrices = np.concatenate(flat)
     fields = np.stack(
         [
             4.0 * local,
@@ -149,7 +156,9 @@
     ).astype(np.float32)
     lane = np.arange(128)
     level = lane % 16
-    rows = np.zeros((32, 128), np.float32)
+    rows = np.zeros((40, 128), np.float32)
+    rows[24:32] = deriv[0][:, None]
+    rows[32:40] = deriv[-1][:, None]
     rows[0] = way
     rows[1] = np.where(level == 0, 1.0, 2.0)
     rows[2] = level < 15
@@ -166,7 +175,8 @@
     return matrices, small, jz, kz, waz
 
 
-M_DZ, M_DX, M_DY, M_LEFT, M_RIGHT, M_JYW, M_KY, M_JY, M_JYT, M_KYT = range(10)
+M_DY, M_RIGHT, M_JYW, M_KY, M_JY, M_JYT, M_KYT = range(768, 768 + 7 * 256, 256)
+M_LEFT = 512
 
 
 def kernel(
@@ -207,8 +217,8 @@
     jz, kz, waz = zcoef
     planes = count // 16
     fields = [small.at[pl.ds(128 * k, 128)] for k in range(4)]
-    rows = small.at[pl.ds(512, 32)]
-    spans = [small.at[pl.ds(544 + 16 * k, 16)] for k in range(3)]
+    rows = small.at[pl.ds(512, 40)]
+    spans = [small.at[pl.ds(552 + 16 * k, 16)] for k in range(3)]
     elem = lax.axis_index("elem")
     sub = lax.axis_index("sub")
     plane = elem // 16
@@ -267,15 +277,31 @@
     def mul(a, b):
         return jnp.dot(a, b, preferred_element_type=jnp.float32)
 
-    def left_dot(index, parts):
+    def rows_of(at, number):
+        return mats[at : at + 128 * number, :]
+
+    def slopes(parts):
         high, low = parts
-        return mul(mats[index, 0], high) + (mul(mats[index, 0], low) + mul(mats[index, 1], high))
-
-    def right_dot(parts, index):
+        big, small_part = mul(rows_of(0, 4), high), mul(rows_of(0, 2), low)
+        along_z = big[0:128] + (big[256:384] + small_part[0:128])
+        along_x = big[128:256] + (big[384:512] + small_part[128:256])
+        return along_z, along_x
+
+    def left_dot(at, parts):
         high, low = parts
-        return mul(high, mats[index, 0]) + (mul(low, mats[index, 0]) + mul(high, mats[index, 1]))
-
-    def near_copies(r, comps):
+        big = mul(rows_of(at, 2), high)
+        return big[0:128] + (big[128:256] + mul(rows_of(at, 1), low))
+
+    def right_dot(parts, at, exact=False):
+        high, low = parts
+        size = high.shape[0]
+        big = mul(jnp.concatenate([high, low], axis=0), rows_of(at, 1))
+        rest = big[size:]
+        if not exact:
+            rest = rest + mul(high, rows_of(at + 128, 1))
+        return big[:size] + rest
+
+    def near_copies(r, comps, part=slice(None)):
         pairs = [
             (co.at[r, 0], cr.at[r, 0]),
             (co.at[r, 1], cr.at[r, 1]),
@@ -295,7 +321,7 @@
                 device_id=near_ids[k],
                 device_id_type=MESH,
             )
-            for k, (src, dst) in enumerate(pairs)
+            for k, (src, dst) in list(enumerate(pairs))[part]
         ]
 
     def take(sem, count_rows):
@@ -305,18 +331,20 @@
     def near_rows(comps):
         return 32 + 48 * comps
 
-    def stage_near(r, comps):
-        for corner, row in enumerate((127, 112, 15, 0)):
+    def stage_corners(r, comps):
+        for corner, row in enumerate(CORNERS):
             tile = jnp.zeros((8, 128), jnp.float32)
             for c in range(comps):
                 tile = jnp.where(sublane == c, work[r, c, row : row + 1, :], tile)
             co[r, corner] = tile
+
+    def stage_faces(r, comps):
         for c in range(comps):
             xs[r, 0, c] = work[r, c, pl.ds(0, 8, stride=16), :]
             xs[r, 1, c] = work[r, c, pl.ds(15, 8, stride=16), :]
 
     def send_near(r, comps, part=slice(None)):
-        for copy in near_copies(r, comps)[part]:
+        for copy in near_copies(r, comps, part):
             copy.start()
 
     def share_y(field):
@@ -347,19 +375,46 @@
                 face = face + jnp.where(sublane == 7, cr[r, 2 + side, c : c + 1, :], 0.0)
                 acc[c, pl.ds(row, 8, stride=16), :] = acc[c, pl.ds(row, 8, stride=16), :] + share_y(face)
 
+    def advect_corners(i):
+        ends = (rows[24:32, :], rows[32:40, :])
+        values, lines = [], []
+        for row in CORNERS:
+            last_z, last_x = int(row >= 112), int(row % 16 == 15)
+            value = jnp.zeros((8, 128), jnp.float32)
+            slope_z, slope_x = value, value
+            for c in range(3):
+                mine = sublane == c
+                value = jnp.where(mine, vel[c, row : row + 1, :], value)
+                line = vel[c, pl.ds(15 * last_x, 8, stride=16), :] * ends[last_z]
+                slope_z = jnp.where(mine, jnp.sum(line, axis=0, keepdims=True), slope_z)
+                at = 112 * last_z + 8 * last_x
+                line = vel[c, at : at + 8, :] * ends[last_x]
+                slope_x = jnp.where(mine, jnp.sum(line, axis=0, keepdims=True), slope_x)
+            values.append(value)
+            lines.append((slope_z, slope_x))
+        slope_y = right_dot(split(jnp.concatenate(values, axis=0)), M_DY)
+        for k, row in enumerate(CORNERS):
+            tile = vel[0, row : row + 1, :] * lines[k][0] + vel[1, row : row + 1, :] * lines[k][1]
+            tile = tile + vel[2, row : row + 1, :] * slope_y[8 * k : 8 * k + 8]
+            co[i, k] = tile * ((2.0 * TIME_STEP) * fields[1][row : row + 1, :])
+
     def advect(i):
         parts = [split(vel[c]) for c in range(3)]
+        stacked = [jnp.concatenate([one[n] for one in parts], axis=0) for n in range(2)]
+        along_y = right_dot(stacked, M_DY)
         for c in range(3):
-            term = vel[0] * left_dot(M_DZ, parts[c])
-            term = term + vel[1] * left_dot(M_DX, parts[c])
-            term = term + vel[2] * right_dot(parts[c], M_DY)
+            along_z, along_x = slopes(parts[c])
+            term = vel[0] * along_z + vel[1] * along_x
+            term = term + vel[2] * along_y[128 * c : 128 * c + 128]
             work[i, c] = term * ((2.0 * TIME_STEP) * fields[1][...])
 
     for copy in loads:
         copy.wait()
+    advect_corners(0)
     advect(0)
-    stage_near(0, 3)
+    stage_faces(0, 3)
     pl.semaphore_wait(barrier, len(partners))
+    send_near(0, 3)
 
     def pass_on(known, ids):
         for one in ids:
@@ -367,8 +422,6 @@
         pl.semaphore_wait(known, len(ids))
 
     def substep(i, carry):
-        send_near(i, 3)
-
         @pl.when(i == 0)
         def _():
             pass_on(known_side, side_ids)
@@ -383,8 +436,11 @@
 
         @pl.when(i < SUBSTEPS - 1)
         def _():
+            advect_corners(i + 1)
+            send_near(i + 1, 3, slice(0, 4))
             advect(i + 1)
-            stage_near(i + 1, 3)
+            stage_faces(i + 1, 3)
+            send_near(i + 1, 3, slice(4, 8))
 
         return carry
 
@@ -400,11 +456,12 @@
                 total = one if total is None else total + one
         return total
 
-    divergence = left_dot(M_DZ, split(vel[0])) + left_dot(M_DX, split(vel[1]))
+    divergence = slopes(split(vel[0]))[0] + slopes(split(vel[1]))[1]
     divergence = divergence + right_dot(split(vel[2]), M_DY)
     source = (-SOURCE_GAIN / 4.0) * fields[0][...] * divergence
     sloc[...] = source
     pres[...] = jnp.zeros_like(source)
+    work[SUBSTEPS, 0] = source
     direct = right_dot(split(source), M_JY).reshape(8, 16, 128)
     for zi in (1, 2):
         row = jnp.sum(weighted(jz, zi, direct) * spans[0][...], axis=0, keepdims=True)
@@ -417,7 +474,7 @@
         return sloc[...] - fields[0][...] * (left_dot(M_LEFT, parts) + right_dot(parts, M_RIGHT))
 
     a_rows = 8 * len(a_ids)
-    b_rows = 24 * len(b_ids)
+    b_rows = 19 * len(b_ids)
 
     def a_copies(it):
         return [
@@ -435,8 +492,8 @@
     def b_copies(it):
         return [
             pltpu.make_async_remote_copy(
-                src_ref=g2.at[it, slot],
-                dst_ref=g2.at[it, slot],
+                src_ref=g2.at[it, slot, pl.ds(0, 19)],
+                dst_ref=g2.at[it, slot, pl.ds(0, 19)],
                 send_sem=b_send.at[it],
                 recv_sem=b_recv.at[it],
                 device_id=one,
@@ -496,11 +553,10 @@
         first = SUBSTEPS + 2 * it
         second = first + 1
         pressure = pres[...]
-        local = minus_laplace(pressure)
-        work[first, 0] = local
+        local = work[first, 0]
         mixed = split(pressure * fields[1][...] + fields[2][...] * local)
         flat = right_dot(mixed, M_JYW).reshape(8, 16, 128)
-        bent = right_dot(mixed, M_KY).reshape(8, 16, 128)
+        bent = right_dot(mixed, M_KY, True).reshape(8, 16, 128)
         tile = jnp.zeros((8, 128), jnp.float32)
         for zi in range(4):
             total = (0.5 * weighted(kz, zi, flat)) * spans[1][...]
@@ -514,7 +570,8 @@
         g1[it, place] = tile
         for copy in a_copies(it):
             copy.start()
-        stage_near(first, 1)
+        stage_corners(first, 1)
+        stage_faces(first, 1)
         send_near(first, 1)
 
         take(a_recv.at[it], a_rows)
@@ -531,7 +588,7 @@
             + some(upper, first_edge),
             (g1[it, 9] + g1[it, 10]) + (g1[it, 11] + g1[it, 12]) + g1[it, 13]
             + (some(lower, first_edge) + some(upper, last_edge)),
-            some(lower, last_edge) + some(upper, base),
+            some(lower, last_edge) + pltpu.roll(some(upper, base), 3, 0),
         ]
         for k in range(3):
             g2[it, slot, 8 * k : 8 * k + 8, :] = pltpu.roll(tops[k], turn, 1)
@@ -542,7 +599,8 @@
         pressure = pressure + fields[2][...] * acc[0]
         pres[...] = pressure
         work[second, 0] = minus_laplace(pressure)
-        stage_near(second, 1)
+        stage_corners(second, 1)
+        stage_faces(second, 1)
         send_near(second, 1)
 
         take(b_recv.at[it], b_rows)
@@ -554,9 +612,10 @@
                 for sy in range(4):
                     one = g2[it, 4 * x + sy, 8 * k : 8 * k + 8, :]
                     if k == 0:
-                        one = one + some(lower, g2[it, 4 * before + sy, 16:24, :])
+                        one = one + some(sublane < 2, g2[it, 4 * before + sy, 16:24, :])
                     else:
-                        one = one + some(upper, g2[it, 4 * after + sy, 16:24, :])
+                        extra = pltpu.roll(g2[it, 4 * after + sy, 16:24, :], 5, 0)
+                        one = one + some(sublane == 7, extra)
                     for n in range(3):
                         at = 8 + 3 * sy + n
                         part = one * rows[at : at + 1, :]
@@ -593,9 +652,15 @@
         image = split(jnp.concatenate(image, axis=0))
         correction = right_dot(interp, M_JYT)
         applied = rows[0:1, :] * right_dot(image, M_JYT)
-        applied = applied + fields[3][...] * right_dot(interp, M_KYT)
+        applied = applied + fields[3][...] * right_dot(interp, M_KYT, True)
         finish_near(second, 1)
-        pres[...] = pres[...] + correction + fields[2][...] * (acc[0] - applied)
+        pressure = pres[...] + correction + fields[2][...] * (acc[0] - applied)
+        pres[...] = pressure
+
+        @pl.when(it < MG_ITERS - 1)
+        def _():
+            work[first + 2, 0] = minus_laplace(pressure)
+
         return carry
 
     lax.fori_loop(0, MG_ITERS, cycle, 0)

time: 61.9 us -> 60.9 us (0.984)
  Pallas kernels: 59.9 us -> 58.9 us
    pallas_call x1, Pallas kernels: 59.9 us -> 58.9 us  [shards(): pl.pallas_call(functools.partial(kernel, (jz, kz, waz), count), out_shape...]
where the time goes in v5:
time: 60.9 us; the launch traced here: 60.8 us
  Pallas kernels  58.9 us (97%)
  local copies, waits for them, and re-layouts  1.31 us (2%)
  between operations  0.64 us (1%)
    pallas_call x1, Pallas kernels, shards(): pl.pallas_call(functools.partial(kernel, (jz, kz, waz), count), out_shape...  58.9 us
    unnamed x2, local copies, waits for them, and re-layouts  1.31 us

profile of v5, /device:TPU:1, one launch (start us, length us, event | category | flops | bytes accessed | tf_op | source)
XLA Modules:
  0.0 60.8 jit_solution(292483813368929709)
XLA Ops:
  0.6 58.9 %shard_map.50 = (f32[3,128,128]{2,1,0:T(8,128)S(1)}, f32[128,128]{1,0:T(8,128)S(1)}) custom-call(f32[3,128,128]{2,1,0:T(8,128)} %bitcast.5, bf16[2560,128]{1,0:T(8,128)(2,1)} %constant.4.clone.mats_in, f32[600,128]{1,0:T(8,128)} %constant.5.clone.small_in), custom_call_target="tpu_custom_call" | custom-call | tf_op jit(solution)/shard_map/pallas_call | solution.py:685
  59.5 0.7 %copy.7 = f32[3,8,16,128]{3,2,1,0:T(8,128)} copy(f32[3,8,16,128]{3,2,1,0:T(8,128)S(1)} %bitcast.3) | data formatting | bytes 393216
  60.2 0.6 %copy.8 = f32[8,16,128]{2,1,0:T(8,128)} copy(f32[8,16,128]{2,1,0:T(8,128)S(1)} %bitcast.4) | data formatting | bytes 131072

commit v6 on v5

--- a/solution.py
+++ b/solution.py
@@ -295,11 +295,10 @@
     def right_dot(parts, at, exact=False):
         high, low = parts
         size = high.shape[0]
-        big = mul(jnp.concatenate([high, low], axis=0), rows_of(at, 1))
-        rest = big[size:]
-        if not exact:
-            rest = rest + mul(high, rows_of(at + 128, 1))
-        return big[:size] + rest
+        rest = mul(low, rows_of(at, 1))
+        if exact:
+            return mul(high, rows_of(at, 1)) + rest
+        return mul(jnp.concatenate([high, high], axis=1), rows_of(at, 2)) + rest
 
     def near_copies(r, comps, part=slice(None)):
         pairs = [
@@ -354,12 +353,14 @@
             + high_lane * pltpu.roll(field, 127, 1)
         )
 
-    def finish_near(r, comps):
+    def begin_near(r, comps):
         for c in range(comps):
             acc[c] = share_y(work[r, c])
             both = acc[c, pl.ds(7, 8, stride=16), :] + acc[c, pl.ds(8, 8, stride=16), :]
             acc[c, pl.ds(7, 8, stride=16), :] = both
             acc[c, pl.ds(8, 8, stride=16), :] = both
+
+    def finish_near(r, comps):
         take(n_recv.at[r], near_rows(comps))
         for c in range(comps):
             for side, row in ((0, 0), (1, 112)):
@@ -430,6 +431,7 @@
         def _():
             pass_on(known_row, row_ids)
 
+        begin_near(i, 3)
         finish_near(i, 3)
         for c in range(3):
             vel[c] = vel[c] - acc[c]
@@ -522,15 +524,30 @@
     def plus(a, factor, b):
         return [x + factor * y for x, y in zip(a, b)]
 
+    def own_planes(k, pair):
+        for half in range(2):
+            ext[k, half, 0:8] = pair[half][count - 8 : count]
+            ext[k, half, 8 : 8 + count] = pair[half]
+            ext[k, half, 8 + count : 16 + count] = pair[half][0:8]
+        body = ext[k, 0, pl.ds(elem + 7, 8), :]
+        wall = ext[k, 1, pl.ds(elem + 7, 8), :]
+        own = rows[20:21, :] * pltpu.roll(body, lax.rem(256 - turn, 128), 1)
+        own = own + rows[21:22, :] * pltpu.roll(wall, lax.rem(208 - turn, 128), 1)
+        return own + rows[22:23, :] * pltpu.roll(wall, lax.rem(159 - turn, 128), 1)
+
     def conjugate(right_side):
         residual = right_side
         image = coarse_apply(residual)
         norm_now = inner(residual, residual)
         energy = inner(residual, image)
         further = coarse_apply(image)
+        planes_of = [own_planes(0, residual)]
         alpha = norm_now / energy
-        direction, moved, twice = residual, image, further
-        solution = [alpha * d for d in direction]
+        inverse = 1.0 / norm_now
+        turned = energy * inverse
+        moved, twice = image, further
+        along = [jnp.ones_like(alpha)]
+        weights = [alpha]
         for sweep in range(1, COARSE_ITERS):
             residual = plus(residual, -alpha, moved)
             image = plus(image, -alpha, twice)
@@ -539,15 +556,19 @@
             more = sweep < COARSE_ITERS - 1
             if more:
                 further = coarse_apply(image)
-            beta = norm_next / norm_now
-            alpha = norm_next / (energy - beta * norm_next / alpha)
-            direction = plus(residual, beta, direction)
-            solution = plus(solution, alpha, direction)
+            planes_of.append(own_planes(sweep, residual))
+            beta = norm_next * inverse
+            energy = energy - (beta * turned) * norm_next
+            alpha = norm_next / energy
+            along = [beta * a for a in along] + [jnp.ones_like(alpha)]
+            weights = [w + alpha * a for w, a in zip(weights + [jnp.zeros_like(alpha)], along)]
             if more:
+                inverse = 1.0 / norm_next
+                turned = energy * inverse
                 moved = plus(image, beta, moved)
                 twice = plus(further, beta, twice)
-            norm_now = norm_next
-        return solution
+        out = [w * one for w, one in zip(weights, planes_of)]
+        return (out[0] + out[1]) + (out[2] + out[3])
 
     def cycle(it, carry):
         first = SUBSTEPS + 2 * it
@@ -573,6 +594,7 @@
         stage_corners(first, 1)
         stage_faces(first, 1)
         send_near(first, 1)
+        begin_near(first, 1)
 
         take(a_recv.at[it], a_rows)
         lower, upper = sublane < 4, sublane >= 4
@@ -602,6 +624,7 @@
         stage_corners(second, 1)
         stage_faces(second, 1)
         send_near(second, 1)
+        begin_near(second, 1)
 
         take(b_recv.at[it], b_rows)
         pieces, walls = [], []
@@ -623,16 +646,7 @@
                 pieces.append(sums[0])
                 walls.append(pltpu.roll(sums[1], 48, 1) + pltpu.roll(sums[2], 97, 1))
         right_side = [jnp.concatenate(pieces, axis=0), jnp.concatenate(walls, axis=0)]
-        answer = conjugate(right_side)
-        for half in range(2):
-            ext[half, 0:8] = answer[half][count - 8 : count]
-            ext[half, 8 : 8 + count] = answer[half]
-            ext[half, 8 + count : 16 + count] = answer[half][0:8]
-        body = ext[0, pl.ds(elem + 7, 8), :]
-        wall = ext[1, pl.ds(elem + 7, 8), :]
-        own = rows[20:21, :] * pltpu.roll(body, lax.rem(256 - turn, 128), 1)
-        own = own + rows[21:22, :] * pltpu.roll(wall, lax.rem(208 - turn, 128), 1)
-        own = own + rows[22:23, :] * pltpu.roll(wall, lax.rem(159 - turn, 128), 1)
+        own = conjugate(right_side)
         vertex = [own[v : v + 1, :] for v in range(4)]
 
         interp, image = [], []
@@ -706,7 +720,7 @@
                 pltpu.VMEM((ROUNDS, 4, 8, 128), f32),
                 pltpu.VMEM((MG_ITERS, 16, 8, 128), f32),
                 pltpu.VMEM((MG_ITERS, 4 * planes, 24, 128), f32),
-                pltpu.VMEM((2, count + 16, 128), f32),
+                pltpu.VMEM((COARSE_ITERS, 2, count + 16, 128), f32),
                 pltpu.VMEM((360, 128), f32),
                 pltpu.SemaphoreType.DMA((3,)),
                 pltpu.SemaphoreType.DMA((ROUNDS,)),

time: 60.9 us -> 60.6 us (level)
  no operation moved by 1% of the time
where the time goes in v6:
time: 60.6 us; the launch traced here: 60.5 us
  Pallas kernels  58.6 us (97%)
  local copies, waits for them, and re-layouts  1.31 us (2%)
  between operations  0.64 us (1%)
    pallas_call x1, Pallas kernels, shards(): pl.pallas_call(functools.partial(kernel, (jz, kz, waz), count), out_shape...  58.6 us
    unnamed x2, local copies, waits for them, and re-layouts  1.31 us

profile of v6, /device:TPU:1, one launch (start us, length us, event | category | flops | bytes accessed | tf_op | source)
XLA Modules:
  0.0 60.5 jit_solution(12776670232137270001)
XLA Ops:
  0.6 58.6 %shard_map.50 = (f32[3,128,128]{2,1,0:T(8,128)S(1)}, f32[128,128]{1,0:T(8,128)S(1)}) custom-call(f32[3,128,128]{2,1,0:T(8,128)} %bitcast.5, bf16[2560,128]{1,0:T(8,128)(2,1)} %constant.4.clone.mats_in, f32[600,128]{1,0:T(8,128)} %constant.5.clone.small_in), custom_call_target="tpu_custom_call" | custom-call | tf_op jit(solution)/shard_map/pallas_call | solution.py:699
  59.2 0.7 %copy.7 = f32[3,8,16,128]{3,2,1,0:T(8,128)} copy(f32[3,8,16,128]{3,2,1,0:T(8,128)S(1)} %bitcast.3) | data formatting | bytes 393216
  59.9 0.6 %copy.8 = f32[8,16,128]{2,1,0:T(8,128)} copy(f32[8,16,128]{2,1,0:T(8,128)S(1)} %bitcast.4) | data formatting | bytes 131072

commit v7 on v6

--- a/solution.py
+++ b/solution.py
@@ -475,14 +475,14 @@
         parts = split(field)
         return sloc[...] - fields[0][...] * (left_dot(M_LEFT, parts) + right_dot(parts, M_RIGHT))
 
-    a_rows = 8 * len(a_ids)
+    a_rows = 4 * len(a_ids)
     b_rows = 19 * len(b_ids)
 
     def a_copies(it):
         return [
             pltpu.make_async_remote_copy(
-                src_ref=g1.at[it, place],
-                dst_ref=g1.at[it, place],
+                src_ref=g1.at[it, place, pl.ds(0, 4)],
+                dst_ref=g1.at[it, place, pl.ds(0, 4)],
                 send_sem=a_send.at[it],
                 recv_sem=a_recv.at[it],
                 device_id=one,
@@ -587,7 +587,7 @@
             row = -jnp.sum(total, axis=0, keepdims=True)
             if zi in (1, 2):
                 row = csrc[zi : zi + 1, :] + row
-            tile = jnp.where(sublane == lax.rem(place + zi + 7, 8), row, tile)
+            tile = jnp.where(sublane == zi, row, tile)
         g1[it, place] = tile
         for copy in a_copies(it):
             copy.start()
@@ -602,13 +602,17 @@
         def some(mask, x):
             return jnp.where(mask, x, 0.0)
 
-        first_edge = g1[it, 6] + g1[it, 7] + g1[it, 8]
-        last_edge = g1[it, 14] + g1[it, 15]
-        base = g1[it, 0]
+        part = []
+        for n in range(16):
+            one = some(lower, g1[it, n])
+            part.append(pltpu.roll(one, (n + 7) % 8, 0) if n % 8 != 1 else one)
+        first_edge = part[6] + part[7] + part[8]
+        last_edge = part[14] + part[15]
+        base = part[0]
         tops = [
-            (g1[it, 1] + g1[it, 2]) + (g1[it, 3] + g1[it, 4]) + (g1[it, 5] + some(lower, base))
+            (part[1] + part[2]) + (part[3] + part[4]) + (part[5] + some(lower, base))
             + some(upper, first_edge),
-            (g1[it, 9] + g1[it, 10]) + (g1[it, 11] + g1[it, 12]) + g1[it, 13]
+            (part[9] + part[10]) + (part[11] + part[12]) + part[13]
             + (some(lower, first_edge) + some(upper, last_edge)),
             some(lower, last_edge) + pltpu.roll(some(upper, base), 3, 0),
         ]

time: 60.6 us -> 59.9 us (0.988)
  Pallas kernels: 58.6 us -> 57.9 us
    pallas_call x1, Pallas kernels: 58.6 us -> 57.9 us  [shards(): pl.pallas_call(functools.partial(kernel, (jz, kz, waz), count), out_shape...]
where the time goes in v7:
time: 59.9 us; the launch traced here: 59.8 us
  Pallas kernels  57.9 us (97%)
  local copies, waits for them, and re-layouts  1.31 us (2%)
  between operations  0.64 us (1%)
    pallas_call x1, Pallas kernels, shards(): pl.pallas_call(functools.partial(kernel, (jz, kz, waz), count), out_shape...  57.9 us
    unnamed x2, local copies, waits for them, and re-layouts  1.31 us

profile of v7, /device:TPU:1, one launch (start us, length us, event | category | flops | bytes accessed | tf_op | source)
XLA Modules:
  0.0 59.8 jit_solution(6058990201093525503)
XLA Ops:
  0.6 57.9 %shard_map.50 = (f32[3,128,128]{2,1,0:T(8,128)S(1)}, f32[128,128]{1,0:T(8,128)S(1)}) custom-call(f32[3,128,128]{2,1,0:T(8,128)} %bitcast.5, bf16[2560,128]{1,0:T(8,128)(2,1)} %constant.4.clone.mats_in, f32[600,128]{1,0:T(8,128)} %constant.5.clone.small_in), custom_call_target="tpu_custom_call" | custom-call | tf_op jit(solution)/shard_map/pallas_call | solution.py:703
  58.5 0.7 %copy.7 = f32[3,8,16,128]{3,2,1,0:T(8,128)} copy(f32[3,8,16,128]{3,2,1,0:T(8,128)S(1)} %bitcast.3) | data formatting | bytes 393216
  59.2 0.6 %copy.8 = f32[8,16,128]{2,1,0:T(8,128)} copy(f32[8,16,128]{2,1,0:T(8,128)S(1)} %bitcast.4) | data formatting | bytes 131072

commit v8 on v7

--- a/solution.py
+++ b/solution.py
@@ -302,10 +302,10 @@
 
     def near_copies(r, comps, part=slice(None)):
         pairs = [
-            (co.at[r, 0], cr.at[r, 0]),
-            (co.at[r, 1], cr.at[r, 1]),
-            (co.at[r, 2], cr.at[r, 2]),
-            (co.at[r, 3], cr.at[r, 3]),
+            (co.at[r, 0, pl.ds(0, comps)], cr.at[r, 0, pl.ds(0, comps)]),
+            (co.at[r, 1, pl.ds(0, comps)], cr.at[r, 1, pl.ds(0, comps)]),
+            (co.at[r, 2, pl.ds(0, comps)], cr.at[r, 2, pl.ds(0, comps)]),
+            (co.at[r, 3, pl.ds(0, comps)], cr.at[r, 3, pl.ds(0, comps)]),
             (work.at[r, pl.ds(0, comps), pl.ds(112, 16)], zr.at[r, 0, pl.ds(0, comps)]),
             (work.at[r, pl.ds(0, comps), pl.ds(0, 16)], zr.at[r, 1, pl.ds(0, comps)]),
             (xs.at[r, 1, pl.ds(0, comps)], xr.at[r, 0, pl.ds(0, comps)]),
@@ -328,7 +328,7 @@
         pltpu.make_async_copy(part, part, sem).wait()
 
     def near_rows(comps):
-        return 32 + 48 * comps
+        return 52 * comps
 
     def stage_corners(r, comps):
         for corner, row in enumerate(CORNERS):

time: 59.9 us -> 59.7 us (level)
  no operation moved by 1% of the time
where the time goes in v8:
time: 59.7 us; the launch traced here: 59.6 us
  Pallas kernels  57.7 us (97%)
  local copies, waits for them, and re-layouts  1.31 us (2%)
  between operations  0.64 us (1%)
    pallas_call x1, Pallas kernels, shards(): pl.pallas_call(functools.partial(kernel, (jz, kz, waz), count), out_shape...  57.7 us
    unnamed x2, local copies, waits for them, and re-layouts  1.31 us

profile of v8, /device:TPU:1, one launch (start us, length us, event | category | flops | bytes accessed | tf_op | source)
XLA Modules:
  0.0 59.6 jit_solution(14189227961574540796)
XLA Ops:
  0.6 57.7 %shard_map.50 = (f32[3,128,128]{2,1,0:T(8,128)S(1)}, f32[128,128]{1,0:T(8,128)S(1)}) custom-call(f32[3,128,128]{2,1,0:T(8,128)} %bitcast.5, bf16[2560,128]{1,0:T(8,128)(2,1)} %constant.4.clone.mats_in, f32[600,128]{1,0:T(8,128)} %constant.5.clone.small_in), custom_call_target="tpu_custom_call" | custom-call | tf_op jit(solution)/shard_map/pallas_call | solution.py:703
  58.3 0.7 %copy.7 = f32[3,8,16,128]{3,2,1,0:T(8,128)} copy(f32[3,8,16,128]{3,2,1,0:T(8,128)S(1)} %bitcast.3) | data formatting | bytes 393216
  59.0 0.6 %copy.8 = f32[8,16,128]{2,1,0:T(8,128)} copy(f32[8,16,128]{2,1,0:T(8,128)S(1)} %bitcast.4) | data formatting | bytes 131072

commit v9 on v8

--- a/solution.py
+++ b/solution.py
@@ -575,6 +575,8 @@
         second = first + 1
         pressure = pres[...]
         local = work[first, 0]
+        stage_corners(first, 1)
+        send_near(first, 1, slice(0, 4))
         mixed = split(pressure * fields[1][...] + fields[2][...] * local)
         flat = right_dot(mixed, M_JYW).reshape(8, 16, 128)
         bent = right_dot(mixed, M_KY, True).reshape(8, 16, 128)
@@ -591,9 +593,8 @@
         g1[it, place] = tile
         for copy in a_copies(it):
             copy.start()
-        stage_corners(first, 1)
         stage_faces(first, 1)
-        send_near(first, 1)
+        send_near(first, 1, slice(4, 8))
         begin_near(first, 1)
 
         take(a_recv.at[it], a_rows)

time: 59.7 us -> 59.7 us (level)
  no operation moved by 1% of the time
where the time goes in v9:
time: 59.7 us; the launch traced here: 59.6 us
  Pallas kernels  57.6 us (96%)
  local copies, waits for them, and re-layouts  1.31 us (2%)
  between operations  0.64 us (1%)
    pallas_call x1, Pallas kernels, shards(): pl.pallas_call(functools.partial(kernel, (jz, kz, waz), count), out_shape...  57.6 us
    unnamed x2, local copies, waits for them, and re-layouts  1.31 us

profile of v9, /device:TPU:1, one launch (start us, length us, event | category | flops | bytes accessed | tf_op | source)
XLA Modules:
  0.0 59.6 jit_solution(2750309463967338056)
XLA Ops:
  0.6 57.6 %shard_map.50 = (f32[3,128,128]{2,1,0:T(8,128)S(1)}, f32[128,128]{1,0:T(8,128)S(1)}) custom-call(f32[3,128,128]{2,1,0:T(8,128)} %bitcast.5, bf16[2560,128]{1,0:T(8,128)(2,1)} %constant.4.clone.mats_in, f32[600,128]{1,0:T(8,128)} %constant.5.clone.small_in), custom_call_target="tpu_custom_call" | custom-call | tf_op jit(solution)/shard_map/pallas_call | solution.py:704
  58.3 0.7 %copy.7 = f32[3,8,16,128]{3,2,1,0:T(8,128)} copy(f32[3,8,16,128]{3,2,1,0:T(8,128)S(1)} %bitcast.3) | data formatting | bytes 393216
  58.9 0.6 %copy.8 = f32[8,16,128]{2,1,0:T(8,128)} copy(f32[8,16,128]{2,1,0:T(8,128)S(1)} %bitcast.4) | data formatting | bytes 131072
